TPU v7x, 256 devices: a whole 4x4x8 slice. The times are simulated.
256 devices in a mesh: dev: 16 (over y, z_lo, core), ha: 16 (over x, z_hi).
Axes of the slice: x: 4, y: 4, z: 8 (z_hi: 4, z_lo: 2; z = z_hi * 2 + z_lo), core: 2. Of those that a mesh axis runs over, the one named last changes fastest.
Arguments:
- image: bfloat16 [32, 64, 256, 256], P(None, 'dev', 'ha'), may hold values from -6 to 6
- kernel_one: bfloat16 [64, 32, 3, 3, 3], replicated, may hold values from -0.21875 to 0.21875
- kernel_two: bfloat16 [128, 64, 3, 3, 3], P('ha'), may hold values from -0.15625 to 0.15625
- cotangent: bfloat16 [128, 16, 64, 64], P('ha', 'dev'), may hold values from -6 to 6
Outputs:
- activation: bfloat16 [128, 16, 64, 64], P('ha', 'dev')
- grad_pooled: bfloat16 [64, 16, 64, 64], P(None, 'dev', 'ha')
- grad_one: float32 [64, 32, 3, 3, 3], replicated
- grad_two: float32 [128, 64, 3, 3, 3], P('ha')
All inputs are finite; a program needn't handle non-finite values.
Results may differ from a plain program's by a relative error of at most 0.02.
Values may be sent and summed in bfloat16 or wider, within the bound.
No kernel may reach another device: no remote copies, remote signals or barrier semaphores. Data moves between devices by JAX's collectives and lax.ppermute only.
A program may use at most 128 MiB of HBM per device.

v0:
```python
import math

import jax
import jax.numpy as jnp
from jax import lax
from jax.experimental import pallas as pl
from jax.experimental.pallas import tpu as pltpu
from jax.sharding import PartitionSpec as P

BF = jnp.bfloat16
F32 = jnp.float32
CELLS_ONE = 524288
CELLS_TWO = 65536
VMEM_LIMIT = 32 * 1024 * 1024


def call(body, out_shape, args, scratch=(), flops=1000000):
    moved = sum(math.prod(s.shape) * s.dtype.itemsize for s in list(out_shape) + list(args))
    return pl.pallas_call(
        body,
        out_shape=out_shape,
        in_specs=[pl.BlockSpec(memory_space=pltpu.VMEM)] * len(args),
        out_specs=[pl.BlockSpec(memory_space=pltpu.VMEM)] * len(out_shape),
        scratch_shapes=scratch,
        compiler_params=pltpu.CompilerParams(vmem_limit_bytes=VMEM_LIMIT),
        cost_estimate=pl.CostEstimate(flops=flops, bytes_accessed=moved, transcendentals=0),
    )(*args)


def shape(dims, dtype):
    return jax.ShapeDtypeStruct(dims, dtype)


def lanes(dims):
    return lax.broadcasted_iota(jnp.int32, dims, len(dims) - 1)


def rows_of(dims):
    return lax.broadcasted_iota(jnp.int32, dims, len(dims) - 2)


def mm(a, b):
    return lax.dot_general(a, b, (((1,), (0,)), ((), ())), preferred_element_type=F32)


def mm_nt(a, b):
    return lax.dot_general(a, b, (((1,), (1,)), ((), ())), preferred_element_type=F32)


def split_mm(a, sel, terms):
    total = None
    for _ in range(terms):
        part = a.astype(BF)
        a = a - part.astype(F32)
        term = mm(part, sel)
        total = term if total is None else total + term
    return total


def edges_body(x_ref, plane_ref, row_ref, corner_ref, last):
    for c in range(32):
        plane_ref[16 * c : 16 * c + 16, :] = x_ref[64 * c + 48 : 64 * c + 64, :]
    for part in range(128):
        block = x_ref[16 * part : 16 * part + 16, :].astype(F32)[8:16]
        for side in range(2):
            last[side, 8 * part : 8 * part + 8, :] = block[:, 128 * side : 128 * side + 128]
    for side in range(2):
        row_ref[:, 128 * side : 128 * side + 128] = last[side, pl.ds(7, 128, stride=8), :].astype(BF)
        corner_ref[:, 128 * side : 128 * side + 128] = last[side, pl.ds(31, 32, stride=32), :].astype(BF)


def pack_body(k_ref, cot_ref, _, out_ref, acc, cots):
    even = is_even("dev")
    pieces = []
    for pair in range(7):
        taps = []
        for t in (2 * pair, 2 * pair + 1):
            high = k_ref[t + 14].astype(F32) if t < 13 else jnp.zeros((8, 64), F32)
            taps.append(jnp.where(even, k_ref[t].astype(F32), high))
        pieces.append(jnp.concatenate(taps, axis=1))
    filters = jnp.concatenate(pieces, axis=1)
    for h in range(16):
        acc[8 * h : 8 * h + 8, 0:896] = filters
    cots[...] = jnp.concatenate([cot_ref[...].astype(F32), jnp.zeros((512, 64), F32)], axis=1)
    for h in range(16):
        for part in range(3):
            two = []
            for row in (4 * h - 1 + 2 * part, 4 * h + 2 * part):
                two.append(cots[pl.ds(row, 8, stride=64), :] if 0 <= row < 64 else jnp.zeros((8, 128), F32))
            at = 896 + 128 * part
            acc[8 * h : 8 * h + 8, at : at + 128] = two[0] + pltpu.roll(two[1], 64, 1)
    out_ref[...] = acc[...].astype(BF)


def parted(value, ev, od, at):
    w_in, n_out = rows_of((256, 256)), lanes((256, 256))
    sel = (w_in == jnp.where(n_out < 128, 2 * n_out, 2 * n_out - 255)).astype(F32).astype(BF)
    both = mm(value, sel)
    ev[at : at + value.shape[0], :] = both[:, :128]
    od[at : at + value.shape[0], :] = both[:, 128:]


def place(out_ref, index, ev, od, start, stride):
    even = ev[pl.ds(start, 32, stride=stride), :]
    odd = od[pl.ds(start, 32, stride=stride), :]
    before = jnp.where(lanes((32, 128)) == 0, 0.0, pltpu.roll(odd, 1, 1))
    out_ref[index, 0:32, :] = before.astype(BF)
    out_ref[index, 32:64, :] = even.astype(BF)
    out_ref[index, 64:96, :] = odd.astype(BF)


def turn_image_body(x_ref, w_ref, own_ref, wt_ref, ev, od):
    for part in range(8):
        parted(x_ref[256 * part : 256 * part + 256, :], ev, od, 256 * part)
    for row in range(64):
        place(own_ref, row, ev, od, row, 64)
    wt_ref[...] = jnp.transpose(w_ref[...].astype(F32), (1, 0)).astype(BF)


def first_layer_body(own_ref, wt_ref, plane_ref, row_ref, corner_ref, slope_ref, pooled_ref, one_ref, other_ref, low_ref, top_ref, ev, od):
    for part in range(2):
        parted(plane_ref[256 * part : 256 * part + 256, :], ev, od, 256 * part)
    parted(row_ref[...], ev, od, 512)
    parted(corner_ref[...], ev, od, 640)
    for r in range(16):
        place(low_ref, r, ev, od, r, 16)
    place(top_ref, 0, ev, od, 640, 1)
    for p in range(4):
        place(top_ref, 1 + p, ev, od, 512 + p, 4)
    weights = wt_ref[...]
    sums = [None] * 4
    for i in range(2):
        for jp in range(4):
            pre = mm(weights, patches_one(own_ref, low_ref, top_ref, i, jp))
            sigma = jax.nn.sigmoid(pre)
            at = (i * 4 + jp) * 256
            slope_ref[:, at : at + 256] = sigma * (1.0 + pre * (1.0 - sigma)) * 0.125
            act = pre * sigma
            both = act[:, :128] + act[:, 128:]
            sums[jp] = both if i == 0 else sums[jp] + both
    k_in, k_out = rows_of((256, 128)), lanes((256, 128))
    fold = ((k_in // 2) == k_out).astype(F32).astype(BF)
    halves = []
    for pair in range(2):
        stacked = jnp.concatenate([sums[2 * pair], sums[2 * pair + 1]], axis=1)
        halves.append(split_mm(stacked, fold, 3) * 0.125)
    pooled = jnp.concatenate(halves, axis=1)
    pooled_ref[...] = pooled.astype(BF)
    even = is_even("ha")
    one_ref[...] = jnp.where(even, halves[1], halves[0]).astype(BF)
    other_ref[...] = jnp.where(even, halves[0], halves[1]).astype(BF)


def patches_one(own_ref, low_ref, top_ref, i, jp):
    def block(a, b):
        if b == 0:
            return top_ref[a]
        return low_ref[b - 1] if a == 0 else own_ref[(a - 1) * 16 + b - 1]

    columns = []
    for j in (2 * jp, 2 * jp + 1):
        columns.append(jnp.concatenate([block(2 * i + a, 2 * j + b) for a in range(3) for b in range(3)], axis=0))
    return jnp.concatenate(columns, axis=1)


def is_even(axis):
    return lax.axis_index(axis) % 2 == 0


def ordered(own_ref, core_ref, cross_ref):
    core, cross = core_ref[...].astype(F32), cross_ref[...].astype(F32)
    even = is_even("dev")
    return (jnp.where(even, cross, core), own_ref[...].astype(F32), jnp.where(even, core, cross))


def shifted(ext):
    width = ext.shape[1]
    kept = width - 128
    column = lanes(ext.shape) & 63
    for e in range(3):
        if e == 0:
            moved = jnp.where(column == 0, 0.0, pltpu.roll(ext, 1, 1))
        elif e == 2:
            moved = jnp.where(column == 63, 0.0, pltpu.roll(ext, width - 1, 1))
        else:
            moved = ext
        yield (0, e), moved[:, 0:kept]
        yield (1, e), pltpu.roll(moved, width - 64, 1)[:, 0:kept]
        yield (2, e), moved[:, 128:width]


def second_layer_body(own_ref, core_ref, cross_ref, w2_ref, a2_ref, patches_ref, act_ref, delta_ref):
    even = is_even("ha")
    for a, plane in enumerate(ordered(own_ref, core_ref, cross_ref)):
        one, other = plane[:, 0:128], plane[:, 384:512]
        plane = jnp.concatenate([jnp.where(even, other, one), plane[:, 128:384], jnp.where(even, one, other)], axis=1)
        for (b, e), value in shifted(plane):
            t = a * 9 + b * 3 + e
            patches_ref[64 * t : 64 * t + 64, :] = value.astype(BF)
    patches_ref[1728:1792, :] = jnp.zeros((64, 384), BF)
    pre = mm(w2_ref[...], patches_ref[...])
    sigma = jax.nn.sigmoid(pre)
    act_ref[...] = pltpu.roll(pre * sigma, 320, 1)[:, 0:256].astype(BF)
    slope = sigma * (1.0 + pre * (1.0 - sigma))
    delta_ref[...] = (a2_ref[:, 896:1280].astype(F32) * slope).astype(BF)


def grad_two_body(delta_ref, patches_ref, keep_ref, give_ref):
    r, o = rows_of((128, 128)), lanes((128, 128))
    order = (o == (r % 16) * 8 + r // 16).astype(F32).astype(BF)
    cell = lanes((128, 384))
    mine = (cell >= 64) & (cell < 320)
    delta = jnp.where(mine, mm(order, delta_ref[...]), 0.0).astype(BF)
    grad = mm_nt(delta, patches_ref[...])
    even = is_even("dev")
    keep_ref[...] = jnp.where(even, grad[:, 0:896], grad[:, 896:1792])
    give_ref[...] = jnp.where(even, grad[:, 896:1792], grad[:, 0:896]).astype(BF)


def turn_filters_body(mine_ref, other_ref, w2_ref, wb_ref):
    even = is_even("dev")
    for pair in range(14):
        at = 128 * (pair % 7)
        mine, other = mine_ref[:, at : at + 128].astype(F32), other_ref[:, at : at + 128].astype(F32)
        block = jnp.where(even, mine, other) if pair < 7 else jnp.where(even, other, mine)
        w2_ref[:, 128 * pair : 128 * pair + 128] = block.astype(BF)
        turned = jnp.transpose(block, (1, 0)).astype(BF)
        wb_ref[:, 256 * pair : 256 * pair + 128] = turned[0:64, :]
        if pair < 13:
            wb_ref[:, 256 * pair + 128 : 256 * pair + 256] = turned[64:128, :]


def backward_body(own_ref, core_ref, cross_ref, wb_ref, slope_ref, image_ref, low_ref, rim_ref, pooled_ref, keep_ref, give_ref, pd, one):
    for a, plane in enumerate(ordered(own_ref, core_ref, cross_ref)):
        for (b, e), value in shifted(plane):
            t = 26 - (a * 9 + b * 3 + e)
            pd[128 * t : 128 * t + 128, :] = value.astype(BF)
    back = mm(wb_ref[...], pd[...])
    for r in range(4):
        turned = back if r == 0 else pltpu.roll(back, 256 - 64 * r, 1)
        pooled_ref[:, r, :] = turned[:, 0:64].astype(BF)
    w_in, n_out = rows_of((128, 256)), lanes((128, 256))
    total = jnp.zeros((64, 1024), F32)
    grown = []
    for pair in range(2):
        grow = (w_in == n_out // 2).astype(F32).astype(BF)
        grown.append(split_mm(back[:, 128 * pair : 128 * pair + 128], grow, 3))
    for i in range(2):
        for jp in range(4):
            row = grown[jp // 2][:, 128 * (jp % 2) : 128 * (jp % 2) + 128]
            at = (i * 4 + jp) * 256
            delta = (jnp.concatenate([row, row], axis=1) * slope_ref[:, at : at + 256]).astype(BF)
            cells = patches_one(image_ref, low_ref, rim_ref, i, jp)
            blank = jnp.zeros((32, 256), BF)
            chunks = []
            for s in range(4):
                chunks += [cells[224 * s : min(224 * s + 224, 864), :], blank]
            chunks.append(blank)
            total = total + mm_nt(delta, jnp.concatenate(chunks, axis=0))
    for s in range(4):
        for quarter in range(4):
            for side in range(2):
                at = 256 * s + 128 * side
                one[side, pl.ds(s * 4 + quarter, 16, stride=16), :] = total[16 * quarter : 16 * quarter + 16, at : at + 128]
    even = is_even("dev")
    for c in range(8):
        for side in range(2):
            at = 128 * side
            first, second = one[side, 32 * c : 32 * c + 16, :], one[side, 32 * c + 16 : 32 * c + 32, :]
            keep_ref[16 * c : 16 * c + 16, at : at + 128] = jnp.where(even, first, second)
            give_ref[16 * c : 16 * c + 16, at : at + 128] = jnp.where(even, second, first).astype(BF)


def sum_chip_body(two_ref, other_two_ref, one_ref, other_one_ref, out_ref):
    out_ref[:, 0:896] = (two_ref[...] + other_two_ref[...].astype(F32)).astype(BF)
    out_ref[:, 896:1152] = (one_ref[...] + other_one_ref[...].astype(F32)).astype(BF)


def sum_depth_body(in_ref, act_ref, out_ref, acc):
    total = in_ref[0:16, :].astype(F32)
    for d in range(1, 8):
        total = total + in_ref[16 * d : 16 * d + 16, :].astype(F32)
    act = act_ref[...].astype(F32)
    acc[...] = jnp.zeros(acc.shape, F32)
    for m in range(7):
        acc[1, pl.ds(m, 16, stride=16), :] = total[:, 128 * m : 128 * m + 128]
    for h in range(16):
        for side in range(2):
            at = 16 * h + 8 * side
            acc[0, at : at + 8, :] = act[8 * h : 8 * h + 8, 128 * side : 128 * side + 128]
    out_ref[:, 256:384] = acc[0].astype(BF)
    out_ref[:, 384:512] = acc[1].astype(BF)
    one = total[:, 896:1152].astype(BF)
    for h in range(16):
        out_ref[16 * h : 16 * h + 16, 0:256] = one


def sum_height_body(in_ref, act_ref, out_ref, acc):
    one, two = None, None
    for h in range(16):
        block = in_ref[16 * h : 16 * h + 16, :].astype(F32)
        one = block[:, 0:256] if h == 0 else one + block[:, 0:256]
        two = block[:, 384:512] if h == 0 else two + block[:, 384:512]
        for r in range(4):
            value = block[8 * (r // 2) : 8 * (r // 2) + 8, 256:384]
            acc[pl.ds(4 * h + r, 8, stride=64), :] = pltpu.roll(value, 64, 1) if r % 2 else value
    act_ref[...] = acc[...][:, 0:64].astype(BF)
    packed = jnp.concatenate([one, two], axis=1).astype(BF)
    for d in range(16):
        out_ref[16 * d : 16 * d + 16, :] = packed


def finish_body(in_ref, one_ref, two_ref, acc):
    for part in range(3):
        acc[part, :, :] = in_ref[:, 128 * part : 128 * part + 128].astype(F32)
    for half in range(2):
        for m in range(7):
            value = acc[2, pl.ds(16 * half + m, 8, stride=32), :] * (1.0 / math.sqrt(CELLS_TWO))
            t = 14 * half + 2 * m
            two_ref[t] = value[:, 0:64]
            if t + 1 < 27:
                two_ref[t + 1] = pltpu.roll(value, 64, 1)[:, 0:64]
    scale = 8.0 / math.sqrt(CELLS_ONE)
    for s in range(4):
        for side in range(2):
            rows = [acc[side, pl.ds(s * 4 + quarter, 16, stride=16), :] for quarter in range(4)]
            turned = jnp.transpose(jnp.concatenate(rows, axis=0), (1, 0)) * scale
            for k in range(4):
                t = 7 * s + 4 * side + k
                if 4 * side + k < 7 and t < 27:
                    one_ref[t] = turned[32 * k : 32 * k + 32, :]


def move(block, axis, step):
    size = lax.axis_size(axis)
    return lax.ppermute(block, axis, [(i, i + step) for i in range(size) if 0 <= i + step < size])


def swap(block, axis, first):
    pairs = [(i, i + 1) for i in range(first, lax.axis_size(axis) - 1, 2)]
    return lax.ppermute(block, axis, pairs + [(j, i) for i, j in pairs])


def exchange(block, axis, groups=None):
    return lax.all_to_all(block, axis, 0, 0, tiled=True, axis_index_groups=groups)


def shards(image, kernel_one, kernel_two, cotangent):
    x = image.reshape(2048, 256)
    k1 = jnp.transpose(kernel_one, (2, 3, 4, 1, 0)).reshape(864, 64)
    k2 = jnp.transpose(kernel_two, (2, 3, 4, 0, 1)).reshape(27, 8, 64)
    cot = cotangent.reshape(512, 64)
    plane, row, corner = call(
        edges_body,
        [shape((512, 256), BF), shape((128, 256), BF), shape((32, 256), BF)],
        [x],
        [pltpu.VMEM((2, 1024, 128), F32)],
    )
    (packed,) = call(
        pack_body,
        [shape((128, 1280), BF)],
        [k2, cot, row],
        [pltpu.VMEM((128, 1280), F32), pltpu.VMEM((512, 128), F32)],
    )
    plane = move(plane, "dev", 1)
    row = move(row, "ha", 1)
    n_dev, n_ha = lax.axis_size("dev"), lax.axis_size("ha")
    corner = lax.ppermute(
        corner,
        ("dev", "ha"),
        [(d * n_ha + h, (d + 1) * n_ha + h + 1) for d in range(n_dev - 1) for h in range(n_ha - 1)],
    )
    a2 = exchange(packed, "ha")
    own, wt = call(
        turn_image_body,
        [shape((64, 96, 128), BF), shape((64, 864), BF)],
        [x, k1],
        [pltpu.VMEM((2048, 128), F32), pltpu.VMEM((2048, 128), F32)],
        flops=300000000,
    )
    slope, pooled, one, other, low, top = call(
        first_layer_body,
        [
            shape((64, 2048), F32),
            shape((64, 256), BF),
            shape((64, 128), BF),
            shape((64, 128), BF),
            shape((16, 96, 128), BF),
            shape((5, 96, 128), BF),
        ],
        [own, wt, plane, row, corner],
        [pltpu.VMEM((672, 128), F32), pltpu.VMEM((672, 128), F32)],
        flops=400000000,
    )
    w2, wb = call(turn_filters_body, [shape((128, 1792), BF), shape((64, 3456), BF)], [a2, swap(a2, "dev", 0)])
    wide = jnp.concatenate([swap(one, "ha", 0), pooled, swap(other, "ha", 1)], axis=1)
    patches, act, delta = call(
        second_layer_body,
        [shape((1792, 384), BF), shape((128, 256), BF), shape((128, 384), BF)],
        [wide, swap(wide, "dev", 0), swap(wide, "dev", 1), w2, a2],
        flops=180000000,
    )
    keep_two, give_two = call(
        grad_two_body, [shape((128, 896), F32), shape((128, 896), BF)], [delta, patches], flops=180000000
    )
    grad_pooled, keep_one, give_one = call(
        backward_body,
        [shape((64, 4, 64), BF), shape((128, 256), F32), shape((128, 256), BF)],
        [delta, swap(delta, "dev", 0), swap(delta, "dev", 1), wb, slope, own, low, top],
        [pltpu.VMEM((3456, 256), BF), pltpu.VMEM((2, 256, 128), F32)],
        flops=400000000,
    )
    (first,) = call(
        sum_chip_body,
        [shape((128, 1152), BF)],
        [keep_two, swap(give_two, "dev", 0), keep_one, swap(give_one, "dev", 0)],
    )
    same_core = [list(range(core, lax.axis_size("dev"), 2)) for core in range(2)]
    (second,) = call(
        sum_depth_body,
        [shape((256, 512), BF)],
        [exchange(first, "dev", same_core), act],
        [pltpu.VMEM((2, 256, 128), F32)],
    )
    activation, third = call(
        sum_height_body,
        [shape((512, 64), BF), shape((256, 384), BF)],
        [exchange(second, "ha")],
        [pltpu.VMEM((512, 128), F32)],
    )
    one, two = call(
        finish_body,
        [shape((27, 32, 64), F32), shape((27, 8, 64), F32)],
        [exchange(third, "dev")],
        [pltpu.VMEM((3, 256, 128), F32)],
    )
    grad_one = jnp.transpose(one.reshape(3, 3, 3, 32, 64), (4, 3, 0, 1, 2))
    grad_two = jnp.transpose(two.reshape(3, 3, 3, 8, 64), (3, 4, 0, 1, 2))
    return (activation.reshape(8, 1, 64, 64), grad_pooled.reshape(64, 1, 4, 64), grad_one, grad_two)


def solution(mesh):
    return jax.shard_map(
        shards,
        mesh=mesh,
        in_specs=(
            P(None, "dev", "ha", None),
            P(),
            P("ha", None, None, None, None),
            P("ha", "dev", None, None),
        ),
        out_specs=(
            P("ha", "dev", None, None),
            P(None, "dev", "ha", None),
            P(),
            P("ha", None, None, None, None),
        ),
        check_vma=False,
    )
```

profile of v0, /device:TPU:1, one launch (start us, length us, event | category | flops | bytes accessed | tf_op | source)
XLA Modules:
  0.0 107.8 jit_solution(9166087619424435984)
XLA Ops:
  0.6 1.2 %copy-done = bf16[32,4,16,256]{3,2,1,0:T(8,128)(2,1)S(1)} copy-done((bf16[32,4,16,256]{3,2,1,0:T(8,128)(2,1)S(1)}, bf16[32,4,16,256]{3,2,1,0:T(8,128)(2,1)}, u32[]{:S(2)}) %copy-start) | copy-done | bytes 1048600
  2.0 1.0 copy-done.3
  3.0 0.8 copy-done.4
  3.8 0.9 shard_map.78
  4.7 11.6 %all-to-all-start = ((bf16[16,8,1280]{2,1,0:T(8,128)(2,1)}), bf16[16,8,1280]{2,1,0:T(8,128)(2,1)S(1)}, u32[]{:S(2)}, u32[]{:S(2)}) async-start(bf16[16,8,1280]{2,1,0:T(8,128)(2,1)} %bitcast.6), calls=%async_computation | async-start | bytes 655360 | tf_op jit(solution)/shard_map/all_to_all | solution.py:345
  16.3 3.5 %collective-permute-start = (bf16[512,256]{1,0:T(8,128)(2,1)S(1)}, bf16[512,256]{1,0:T(8,128)(2,1)S(1)}, u32[]{:S(2)}, u32[]{:S(2)}) collective-permute-start(bf16[512,256]{1,0:T(8,128)(2,1)S(1)} %get-tuple-element.31), channel_id=1, source_target_pairs={{0,16},{16,32},{32,48},{48,64},{64,80},{80,96},{96,112},{112,128},... | collective-permute-start | bytes 786440 | tf_op jit(solution)/shard_map/ppermute | solution.py:336
  19.8 4.4 %collective-permute-start.1 = (bf16[128,256]{1,0:T(8,128)(2,1)S(1)}, bf16[128,256]{1,0:T(8,128)(2,1)S(1)}, u32[]{:S(2)}, u32[]{:S(2)}) collective-permute-start(bf16[128,256]{1,0:T(8,128)(2,1)S(1)} %get-tuple-element.32._), channel_id=1, source_target_pairs={{0,1},{1,2},{2,3},{3,4},{4,5},{5,6},{6,7},{7,8},{8,9},{9,10},{10,1... | collective-permute-start | bytes 196616 | tf_op jit(solution)/shard_map/ppermute | solution.py:336
  24.3 5.2 %collective-permute-start.2 = (bf16[32,256]{1,0:T(8,128)(2,1)S(1)}, bf16[32,256]{1,0:T(8,128)(2,1)S(1)}, u32[]{:S(2)}, u32[]{:S(2)}) collective-permute-start(bf16[32,256]{1,0:T(8,128)(2,1)S(1)} %get-tuple-element.33), channel_id=1, source_target_pairs={{0,17},{1,18},{2,19},{3,20},{4,21},{5,22},{6,23},{7,24},{8,25},{9,... | collective-permute-start | bytes 49160 | tf_op jit(solution)/shard_map/ppermute | solution.py:368
  29.5 1.7 %shard_map.75 = (bf16[64,96,128]{2,1,0:T(8,128)(2,1)S(1)}, bf16[64,864]{1,0:T(8,128)(2,1)S(1)}) custom-call(bf16[2048,256]{1,0:T(8,128)(2,1)S(1)} %bitcast.29, bf16[864,64]{1,0:T(8,128)(2,1)S(1)} %bitcast.38), custom_call_target="tpu_custom_call" | custom-call | flops 300000000 | bytes 2842624 | tf_op jit(solution)/shard_map/pallas_call | solution.py:19
  31.2 1.4 %shard_map.77 = (f32[64,2048]{1,0:T(8,128)S(1)}, bf16[64,256]{1,0:T(8,128)(2,1)S(1)}, bf16[64,128]{1,0:T(8,128)(2,1)S(1)}, bf16[64,128]{1,0:T(8,128)(2,1)S(1)}, ...) custom-call(bf16[64,96,128]{2,1,0:T(8,128)(2,1)S(1)} %get-tuple-element.29.own_ref.image_ref, ...), custom_call_target="tpu_custom_call" | custom-call | flops 400000000 | bytes 3133440 | tf_op jit(solution)/shard_map/pallas_call | solution.py:19
  32.6 2.7 %collective-permute-start.3 = (bf16[64,128]{1,0:T(8,128)(2,1)S(1)}, bf16[64,128]{1,0:T(8,128)(2,1)S(1)}, u32[]{:S(2)}, u32[]{:S(2)}) collective-permute-start(bf16[64,128]{1,0:T(8,128)(2,1)S(1)} %get-tuple-element.34), channel_id=1, source_target_pairs={{0,1},{2,3},{4,5},{6,7},{8,9},{10,11},{12,13},{14,15},{1,0},{3,2},... | collective-permute-start | bytes 49160 | tf_op jit(solution)/shard_map/ppermute | solution.py:341
  36.4 4.9 %collective-permute-start.6 = (bf16[64,512]{1,0:T(8,128)(2,1)S(1)}, bf16[64,512]{1,0:T(8,128)(2,1)S(1)}, u32[]{:S(2)}, u32[]{:S(2)}) collective-permute-start(bf16[64,512]{1,0:T(8,128)(2,1)S(1)} %constant_dynamic-update-slice_fusion.own_ref), channel_id=1, source_target_pairs={{16,32},{48,64},{80,96},{112,128},{144,160},{176,192},{208,224},{3... | collective-permute-start | bytes 196616 | tf_op jit(solution)/shard_map/ppermute | solution.py:341
  41.7 1.9 %collective-permute-done.6.cross_ref = bf16[64,512]{1,0:T(8,128)(2,1)S(1)} collective-permute-done((bf16[64,512]{1,0:T(8,128)(2,1)S(1)}, bf16[64,512]{1,0:T(8,128)(2,1)S(1)}, u32[]{:S(2)}, u32[]{:S(2)}) %collective-permute-start.6) | collective-permute-done | bytes 65568 | tf_op jit(solution)/shard_map/ppermute | solution.py:341
  43.6 0.9 shard_map.80
  44.5 0.7 shard_map.81
  45.3 3.5 %collective-permute-start.10 = (bf16[128,384]{1,0:T(8,128)(2,1)S(1)}, bf16[128,384]{1,0:T(8,128)(2,1)S(1)}, u32[]{:S(2)}, u32[]{:S(2)}) collective-permute-start(bf16[128,384]{1,0:T(8,128)(2,1)S(1)} %get-tuple-element.38.delta_ref.own_ref), channel_id=1, source_target_pairs={{16,32},{48,64},{80,96},{112,128},{144,160},{176,192},{208,224},{3... | collective-permute-start | bytes 294920 | tf_op jit(solution)/shard_map/ppermute | solution.py:341
  48.9 2.4 %collective-permute-done.10.cross_ref = bf16[128,384]{1,0:T(8,128)(2,1)S(1)} collective-permute-done((bf16[128,384]{1,0:T(8,128)(2,1)S(1)}, bf16[128,384]{1,0:T(8,128)(2,1)S(1)}, u32[]{:S(2)}, u32[]{:S(2)}) %collective-permute-start.10) | collective-permute-done | bytes 98336 | tf_op jit(solution)/shard_map/ppermute | solution.py:341
  51.2 2.2 %shard_map.82 = (bf16[64,4,64]{2,1,0:T(4,128)(2,1)}, f32[128,256]{1,0:T(8,128)S(1)}, bf16[128,256]{1,0:T(8,128)(2,1)S(1)}) custom-call(bf16[128,384]{1,0:T(8,128)(2,1)S(1)} %get-tuple-element.38.delta_ref.own_ref, bf16[128,384]{1,0:T(8,128)(2,1)S(1)} %collective-permute-done.9.core_ref, bf16[128,384]{1,0:T(8,128)(2,1)S(1)} %collective-permute-done.10.cross_ref, ...), custom_call_target="tpu_custom_call" | custom-call | flops 400000000 | bytes 3579904 | tf_op jit(solution)/shard_map/pallas_call | solution.py:19
  53.6 1.2 %collective-permute-done.11.other_one_ref = bf16[128,256]{1,0:T(8,128)(2,1)S(1)} collective-permute-done((bf16[128,256]{1,0:T(8,128)(2,1)S(1)}, bf16[128,256]{1,0:T(8,128)(2,1)S(1)}, u32[]{:S(2)}, u32[]{:S(2)}) %collective-permute-start.11) | collective-permute-done | bytes 65568 | tf_op jit(solution)/shard_map/ppermute | solution.py:341
  54.9 13.4 %all_to_all.44 = bf16[8,16,1152]{2,1,0:T(8,128)(2,1)S(1)} all-to-all(bf16[8,16,1152]{2,1,0:T(8,128)(2,1)S(1)} %bitcast.34), channel_id=1, replica_groups={{0,32,64,96,128,160,192,224},{16,48,80,112,144,176,208,240},{1,33,65,97..., dimensions={0} | all-to-all | bytes 589824 | tf_op jit(solution)/shard_map/all_to_all | solution.py:345
  68.4 25.5 %all_to_all.45 = bf16[16,16,512]{2,1,0:T(8,128)(2,1)S(1)} all-to-all(bf16[16,16,512]{2,1,0:T(8,128)(2,1)S(1)} %bitcast.36), channel_id=1, replica_groups=mesh['dev'=16,'ha'=16] {'ha'}, dimensions={0} | all-to-all | bytes 524288 | tf_op jit(solution)/shard_map/all_to_all | solution.py:345
  93.9 0.9 shard_map.85
  94.8 12.0 %all_to_all.46 = bf16[16,16,384]{2,1,0:T(8,128)(2,1)S(1)} all-to-all(bf16[16,16,384]{2,1,0:T(8,128)(2,1)S(1)} %bitcast.39), channel_id=1, replica_groups=mesh['dev'=16,'ha'=16] {'dev'}, dimensions={0} | all-to-all | bytes 393216 | tf_op jit(solution)/shard_map/all_to_all | solution.py:345
  106.8 1.0 shard_map.86
  (30 shorter events, 2.1 us)
Async XLA Ops:
  0.6 1.2 %copy-start = (bf16[32,4,16,256]{3,2,1,0:T(8,128)(2,1)S(1)}, bf16[32,4,16,256]{3,2,1,0:T(8,128)(2,1)}, u32[]{:S(2)}) copy-start(bf16[32,4,16,256]{3,2,1,0:T(8,128)(2,1)} %param.4) | copy-start | bytes 3145732
  1.9 27.6 %copy-start.1 = (bf16[32,4,16,256]{3,2,1,0:T(8,128)(2,1)S(1)}, bf16[32,4,16,256]{3,2,1,0:T(8,128)(2,1)}, u32[]{:S(2)}) copy-start(bf16[32,4,16,256]{3,2,1,0:T(8,128)(2,1)} %param.4) | copy-start | bytes 3145732
  1.9 27.6 %copy-start.2 = (bf16[64,32,3,3,3]{0,1,4,3,2:T(8,128)(2,1)S(1)}, bf16[64,32,3,3,3]{0,1,4,3,2:T(8,128)(2,1)}, u32[]{:S(2)}) copy-start(bf16[64,32,3,3,3]{0,1,4,3,2:T(8,128)(2,1)} %param.5) | copy-start | bytes 331780
  2.0 1.0 copy-start.3
  3.0 0.8 copy-start.4
  4.7 31.2 %all-to-all-start = ((bf16[16,8,1280]{2,1,0:T(8,128)(2,1)}), bf16[16,8,1280]{2,1,0:T(8,128)(2,1)S(1)}, u32[]{:S(2)}, u32[]{:S(2)}) async-start(bf16[16,8,1280]{2,1,0:T(8,128)(2,1)} %bitcast.6), calls=%async_computation | async-start | bytes 655360 | tf_op jit(solution)/shard_map/all_to_all | solution.py:345
  16.3 14.9 %collective-permute-start = (bf16[512,256]{1,0:T(8,128)(2,1)S(1)}, bf16[512,256]{1,0:T(8,128)(2,1)S(1)}, u32[]{:S(2)}, u32[]{:S(2)}) collective-permute-start(bf16[512,256]{1,0:T(8,128)(2,1)S(1)} %get-tuple-element.31), channel_id=1, source_target_pairs={{0,16},{16,32},{32,48},{48,64},{64,80},{80,96},{96,112},{112,128},... | collective-permute-start | bytes 786440 | tf_op jit(solution)/shard_map/ppermute | solution.py:336
  19.8 11.4 %collective-permute-start.1 = (bf16[128,256]{1,0:T(8,128)(2,1)S(1)}, bf16[128,256]{1,0:T(8,128)(2,1)S(1)}, u32[]{:S(2)}, u32[]{:S(2)}) collective-permute-start(bf16[128,256]{1,0:T(8,128)(2,1)S(1)} %get-tuple-element.32._), channel_id=1, source_target_pairs={{0,1},{1,2},{2,3},{3,4},{4,5},{5,6},{6,7},{7,8},{8,9},{9,10},{10,1... | collective-permute-start | bytes 196616 | tf_op jit(solution)/shard_map/ppermute | solution.py:336
  24.3 6.9 %collective-permute-start.2 = (bf16[32,256]{1,0:T(8,128)(2,1)S(1)}, bf16[32,256]{1,0:T(8,128)(2,1)S(1)}, u32[]{:S(2)}, u32[]{:S(2)}) collective-permute-start(bf16[32,256]{1,0:T(8,128)(2,1)S(1)} %get-tuple-element.33), channel_id=1, source_target_pairs={{0,17},{1,18},{2,19},{3,20},{4,21},{5,22},{6,23},{7,24},{8,25},{9,... | collective-permute-start | bytes 49160 | tf_op jit(solution)/shard_map/ppermute | solution.py:368
  32.6 3.8 %collective-permute-start.3 = (bf16[64,128]{1,0:T(8,128)(2,1)S(1)}, bf16[64,128]{1,0:T(8,128)(2,1)S(1)}, u32[]{:S(2)}, u32[]{:S(2)}) collective-permute-start(bf16[64,128]{1,0:T(8,128)(2,1)S(1)} %get-tuple-element.34), channel_id=1, source_target_pairs={{0,1},{2,3},{4,5},{6,7},{8,9},{10,11},{12,13},{14,15},{1,0},{3,2},... | collective-permute-start | bytes 49160 | tf_op jit(solution)/shard_map/ppermute | solution.py:341
  35.3 1.1 %collective-permute-start.4 = (bf16[64,128]{1,0:T(8,128)(2,1)S(1)}, bf16[64,128]{1,0:T(8,128)(2,1)S(1)}, u32[]{:S(2)}, u32[]{:S(2)}) collective-permute-start(bf16[64,128]{1,0:T(8,128)(2,1)S(1)} %get-tuple-element.36), channel_id=1, source_target_pairs={{1,2},{3,4},{5,6},{7,8},{9,10},{11,12},{13,14},{2,1},{4,3},{6,5},{... | collective-permute-start | bytes 49160 | tf_op jit(solution)/shard_map/ppermute | solution.py:341
  35.9 5.5 %collective-permute-start.7 = (bf16[128,1280]{1,0:T(8,128)(2,1)S(1)}, bf16[128,1280]{1,0:T(8,128)(2,1)S(1)}, u32[]{:S(2)}, u32[]{:S(2)}) collective-permute-start(bf16[128,1280]{1,0:T(8,128)(2,1)S(1)} %bitcast.30), channel_id=1, source_target_pairs={{0,16},{32,48},{64,80},{96,112},{128,144},{160,176},{192,208},{224... | collective-permute-start | bytes 983048 | tf_op jit(solution)/shard_map/ppermute | solution.py:341
  36.4 7.2 %collective-permute-start.6 = (bf16[64,512]{1,0:T(8,128)(2,1)S(1)}, bf16[64,512]{1,0:T(8,128)(2,1)S(1)}, u32[]{:S(2)}, u32[]{:S(2)}) collective-permute-start(bf16[64,512]{1,0:T(8,128)(2,1)S(1)} %constant_dynamic-update-slice_fusion.own_ref), channel_id=1, source_target_pairs={{16,32},{48,64},{80,96},{112,128},{144,160},{176,192},{208,224},{3... | collective-permute-start | bytes 196616 | tf_op jit(solution)/shard_map/ppermute | solution.py:341
  41.3 2.3 %collective-permute-start.5 = (bf16[64,512]{1,0:T(8,128)(2,1)S(1)}, bf16[64,512]{1,0:T(8,128)(2,1)S(1)}, u32[]{:S(2)}, u32[]{:S(2)}) collective-permute-start(bf16[64,512]{1,0:T(8,128)(2,1)S(1)} %constant_dynamic-update-slice_fusion.own_ref), channel_id=1, source_target_pairs={{0,16},{32,48},{64,80},{96,112},{128,144},{160,176},{192,208},{224... | collective-permute-start | bytes 196616 | tf_op jit(solution)/shard_map/ppermute | solution.py:341
  45.2 9.6 %collective-permute-start.8 = (bf16[128,896]{1,0:T(8,128)(2,1)S(1)}, bf16[128,896]{1,0:T(8,128)(2,1)S(1)}, u32[]{:S(2)}, u32[]{:S(2)}) collective-permute-start(bf16[128,896]{1,0:T(8,128)(2,1)S(1)} %get-tuple-element.41), channel_id=1, source_target_pairs={{0,16},{32,48},{64,80},{96,112},{128,144},{160,176},{192,208},{224... | collective-permute-start | bytes 688136 | tf_op jit(solution)/shard_map/ppermute | solution.py:341
  45.3 5.9 %collective-permute-start.10 = (bf16[128,384]{1,0:T(8,128)(2,1)S(1)}, bf16[128,384]{1,0:T(8,128)(2,1)S(1)}, u32[]{:S(2)}, u32[]{:S(2)}) collective-permute-start(bf16[128,384]{1,0:T(8,128)(2,1)S(1)} %get-tuple-element.38.delta_ref.own_ref), channel_id=1, source_target_pairs={{16,32},{48,64},{80,96},{112,128},{144,160},{176,192},{208,224},{3... | collective-permute-start | bytes 294920 | tf_op jit(solution)/shard_map/ppermute | solution.py:341
  48.8 2.5 %collective-permute-start.9 = (bf16[128,384]{1,0:T(8,128)(2,1)S(1)}, bf16[128,384]{1,0:T(8,128)(2,1)S(1)}, u32[]{:S(2)}, u32[]{:S(2)}) collective-permute-start(bf16[128,384]{1,0:T(8,128)(2,1)S(1)} %get-tuple-element.38.delta_ref.own_ref), channel_id=1, source_target_pairs={{0,16},{32,48},{64,80},{96,112},{128,144},{160,176},{192,208},{224... | collective-permute-start | bytes 294920 | tf_op jit(solution)/shard_map/ppermute | solution.py:341
  53.5 1.3 %collective-permute-start.11 = (bf16[128,256]{1,0:T(8,128)(2,1)S(1)}, bf16[128,256]{1,0:T(8,128)(2,1)S(1)}, u32[]{:S(2)}, u32[]{:S(2)}) collective-permute-start(bf16[128,256]{1,0:T(8,128)(2,1)S(1)} %get-tuple-element.47), channel_id=1, source_target_pairs={{0,16},{32,48},{64,80},{96,112},{128,144},{160,176},{192,208},{224... | collective-permute-start | bytes 196616 | tf_op jit(solution)/shard_map/ppermute | solution.py:341
where the time goes:
time: 108 us
  blocking collectives  51 us (47%)
  starting transfers between devices  36.8 us (34%)
  Pallas kernels  10.2 us (9%)
  waiting for transfers between devices  5.93 us (5%)
  local copies, waits for them, and re-layouts  3.04 us (3%)
    all_to_all x3, blocking collectives, exchange(): lax.all_to_all(block, axis, 0, 0, tiled=True, axis_index_groups=groups)  51 us
    ppermute x9, starting transfers between devices, swap(): return lax.ppermute(block, axis, pairs + [(j, i) for i, j in pairs])  12.1 us
    all_to_all x1, starting transfers between devices, exchange(): lax.all_to_all(block, axis, 0, 0, tiled=True, axis_index_groups=groups)  11.6 us
    pallas_call x12, Pallas kernels, call(): pl.pallas_call(body, out_shape=out_shape, in_specs=[pl.BlockSpec(memory_s...  10.2 us
    ppermute x2, starting transfers between devices, move(): lax.ppermute(block, axis, [(i, i + step) for i in range(size) if 0 <= i +...  7.93 us
    ppermute x9, waiting for transfers between devices, swap(): return lax.ppermute(block, axis, pairs + [(j, i) for i, j in pairs])  5.92 us
    ppermute x1, starting transfers between devices, shards(): lax.ppermute(corner, ('dev', 'ha'), [(d * n_ha + h, (d + 1) * n_ha + h +...  5.21 us
    unnamed x12, local copies, waits for them, and re-layouts  3.02 us
  transfers between devices with their start and end apart: 13, of which 4 were waited for; matrix products, arithmetic and copies ran while one was open for 0% of the time, Pallas kernels for 5%

commit v1 on v0

--- a/solution.py
+++ b/solution.py
@@ -14,15 +14,15 @@
 VMEM_LIMIT = 32 * 1024 * 1024
 
 
-def call(body, out_shape, args, scratch=(), flops=1000000):
+def call(body, out_shape, args, scratch=(), flops=1000000, space=pltpu.VMEM, limit=VMEM_LIMIT):
     moved = sum(math.prod(s.shape) * s.dtype.itemsize for s in list(out_shape) + list(args))
     return pl.pallas_call(
         body,
         out_shape=out_shape,
-        in_specs=[pl.BlockSpec(memory_space=pltpu.VMEM)] * len(args),
+        in_specs=[pl.BlockSpec(memory_space=space)] * len(args),
         out_specs=[pl.BlockSpec(memory_space=pltpu.VMEM)] * len(out_shape),
         scratch_shapes=scratch,
-        compiler_params=pltpu.CompilerParams(vmem_limit_bytes=VMEM_LIMIT),
+        compiler_params=pltpu.CompilerParams(vmem_limit_bytes=limit),
         cost_estimate=pl.CostEstimate(flops=flops, bytes_accessed=moved, transcendentals=0),
     )(*args)
 
@@ -57,19 +57,12 @@
     return total
 
 
-def edges_body(x_ref, plane_ref, row_ref, corner_ref, last):
-    for c in range(32):
-        plane_ref[16 * c : 16 * c + 16, :] = x_ref[64 * c + 48 : 64 * c + 64, :]
-    for part in range(128):
-        block = x_ref[16 * part : 16 * part + 16, :].astype(F32)[8:16]
-        for side in range(2):
-            last[side, 8 * part : 8 * part + 8, :] = block[:, 128 * side : 128 * side + 128]
-    for side in range(2):
-        row_ref[:, 128 * side : 128 * side + 128] = last[side, pl.ds(7, 128, stride=8), :].astype(BF)
-        corner_ref[:, 128 * side : 128 * side + 128] = last[side, pl.ds(31, 32, stride=32), :].astype(BF)
-
-
-def pack_body(k_ref, cot_ref, _, out_ref, acc, cots):
+def pack_body(x_hbm, k_hbm, cot_hbm, plane_ref, row_ref, corner_ref, out_ref, x_ref, k_ref, cot_ref, last, acc, cots, sems):
+    copies = []
+    for i, (src, dst) in enumerate([(x_hbm, x_ref), (k_hbm, k_ref), (cot_hbm, cot_ref)]):
+        copies.append(pltpu.make_async_copy(src, dst, sems.at[i]))
+        copies[i].start()
+    copies[1].wait()
     even = is_even("dev")
     pieces = []
     for pair in range(7):
@@ -81,6 +74,7 @@
     filters = jnp.concatenate(pieces, axis=1)
     for h in range(16):
         acc[8 * h : 8 * h + 8, 0:896] = filters
+    copies[2].wait()
     cots[...] = jnp.concatenate([cot_ref[...].astype(F32), jnp.zeros((512, 64), F32)], axis=1)
     for h in range(16):
         for part in range(3):
@@ -90,6 +84,17 @@
             at = 896 + 128 * part
             acc[8 * h : 8 * h + 8, at : at + 128] = two[0] + pltpu.roll(two[1], 64, 1)
     out_ref[...] = acc[...].astype(BF)
+    copies[0].wait()
+    for c in range(32):
+        plane_ref[16 * c : 16 * c + 16, :] = x_ref[64 * c + 48 : 64 * c + 64, :]
+    for part in range(128):
+        block = x_ref[16 * part : 16 * part + 16, :].astype(F32)[8:16]
+        for side in range(2):
+            last[side, 8 * part : 8 * part + 8, :] = block[:, 128 * side : 128 * side + 128]
+    for side in range(2):
+        at = 128 * side
+        row_ref[:, at : at + 128] = last[side, pl.ds(7, 128, stride=8), :].astype(BF)
+        corner_ref[:, at : at + 128] = last[side, pl.ds(31, 32, stride=32), :].astype(BF)
 
 
 def parted(value, ev, od, at):
@@ -117,7 +122,7 @@
     wt_ref[...] = jnp.transpose(w_ref[...].astype(F32), (1, 0)).astype(BF)
 
 
-def first_layer_body(own_ref, wt_ref, plane_ref, row_ref, corner_ref, slope_ref, pooled_ref, one_ref, other_ref, low_ref, top_ref, ev, od):
+def first_layer_body(own_ref, wt_ref, plane_ref, row_ref, corner_ref, slope_ref, pooled_ref, low_ref, top_ref, ev, od):
     for part in range(2):
         parted(plane_ref[256 * part : 256 * part + 256, :], ev, od, 256 * part)
     parted(row_ref[...], ev, od, 512)
@@ -146,9 +151,6 @@
         halves.append(split_mm(stacked, fold, 3) * 0.125)
     pooled = jnp.concatenate(halves, axis=1)
     pooled_ref[...] = pooled.astype(BF)
-    even = is_even("ha")
-    one_ref[...] = jnp.where(even, halves[1], halves[0]).astype(BF)
-    other_ref[...] = jnp.where(even, halves[0], halves[1]).astype(BF)
 
 
 def patches_one(own_ref, low_ref, top_ref, i, jp):
@@ -165,12 +167,6 @@
 
 def is_even(axis):
     return lax.axis_index(axis) % 2 == 0
-
-
-def ordered(own_ref, core_ref, cross_ref):
-    core, cross = core_ref[...].astype(F32), cross_ref[...].astype(F32)
-    even = is_even("dev")
-    return (jnp.where(even, cross, core), own_ref[...].astype(F32), jnp.where(even, core, cross))
 
 
 def shifted(ext):
@@ -189,20 +185,58 @@
         yield (2, e), moved[:, 128:width]
 
 
-def second_layer_body(own_ref, core_ref, cross_ref, w2_ref, a2_ref, patches_ref, act_ref, delta_ref):
-    even = is_even("ha")
-    for a, plane in enumerate(ordered(own_ref, core_ref, cross_ref)):
-        one, other = plane[:, 0:128], plane[:, 384:512]
-        plane = jnp.concatenate([jnp.where(even, other, one), plane[:, 128:384], jnp.where(even, one, other)], axis=1)
+def rims_body(own_ref, other_ref, out_ref):
+    bottom = is_even("ha") == is_even("dev")
+    for k, ref in enumerate((own_ref, other_ref)):
+        value = ref[...].astype(F32)
+        out_ref[64 * k : 64 * k + 64, :] = jnp.where(bottom, value[:, 128:256], value[:, 0:128]).astype(BF)
+
+
+def widen_body(own_ref, other_ref, mine_ref, core_ref, a2_ref, out_ref):
+    swapped = is_even("ha") == is_even("dev")
+    mine, core = mine_ref[...].astype(F32), core_ref[...].astype(F32)
+    for k, ref in enumerate((own_ref, other_ref)):
+        here, there = mine[64 * k : 64 * k + 64], core[64 - 64 * k : 128 - 64 * k]
+        out_ref[64 * k : 64 * k + 64, 0:128] = jnp.where(swapped, there, here).astype(BF)
+        out_ref[64 * k : 64 * k + 64, 128:384] = ref[...]
+        out_ref[64 * k : 64 * k + 64, 384:512] = jnp.where(swapped, here, there).astype(BF)
+    out_ref[:, 512:896] = a2_ref[:, 896:1280]
+
+
+def second_layer_body(pair_ref, cross_ref, core_ref, w2_ref, other_ref, patches_ref, act_ref, delta_ref):
+    even = is_even("dev")
+
+    def planes(ref):
+        return ref[0:64, 0:512].astype(F32), ref[64:128, 0:512].astype(F32)
+
+    own, other = planes(pair_ref)
+    near, far = planes(cross_ref)
+    beyond = core_ref[0:64, 0:512].astype(F32)
+    ordered = (
+        jnp.where(even, far, beyond),
+        jnp.where(even, near, other),
+        own,
+        jnp.where(even, other, near),
+        jnp.where(even, beyond, far),
+    )
+    for a, plane in enumerate(ordered):
         for (b, e), value in shifted(plane):
             t = a * 9 + b * 3 + e
             patches_ref[64 * t : 64 * t + 64, :] = value.astype(BF)
-    patches_ref[1728:1792, :] = jnp.zeros((64, 384), BF)
-    pre = mm(w2_ref[...], patches_ref[...])
-    sigma = jax.nn.sigmoid(pre)
-    act_ref[...] = pltpu.roll(pre * sigma, 320, 1)[:, 0:256].astype(BF)
-    slope = sigma * (1.0 + pre * (1.0 - sigma))
-    delta_ref[...] = (a2_ref[:, 896:1280].astype(F32) * slope).astype(BF)
+    patches_ref[2880:2944, :] = jnp.zeros((64, 384), BF)
+    cot_cross, cot_core = cross_ref[:, 512:896].astype(F32), other_ref[:, 896:1280].astype(F32)
+    cots = (
+        jnp.where(even, cot_cross, cot_core),
+        pair_ref[:, 512:896].astype(F32),
+        jnp.where(even, cot_core, cot_cross),
+    )
+    for p in range(3):
+        pre = mm(w2_ref[...], patches_ref[576 * p : 576 * p + 1792, :])
+        sigma = jax.nn.sigmoid(pre)
+        if p == 1:
+            act_ref[...] = pltpu.roll(pre * sigma, 320, 1)[:, 0:256].astype(BF)
+        slope = sigma * (1.0 + pre * (1.0 - sigma))
+        delta_ref[128 * p : 128 * p + 128, :] = (cots[p] * slope).astype(BF)
 
 
 def grad_two_body(delta_ref, patches_ref, keep_ref, give_ref):
@@ -210,8 +244,8 @@
     order = (o == (r % 16) * 8 + r // 16).astype(F32).astype(BF)
     cell = lanes((128, 384))
     mine = (cell >= 64) & (cell < 320)
-    delta = jnp.where(mine, mm(order, delta_ref[...]), 0.0).astype(BF)
-    grad = mm_nt(delta, patches_ref[...])
+    delta = jnp.where(mine, mm(order, delta_ref[128:256, :]), 0.0).astype(BF)
+    grad = mm_nt(delta, patches_ref[576:2368, :])
     even = is_even("dev")
     keep_ref[...] = jnp.where(even, grad[:, 0:896], grad[:, 896:1792])
     give_ref[...] = jnp.where(even, grad[:, 896:1792], grad[:, 0:896]).astype(BF)
@@ -230,9 +264,9 @@
             wb_ref[:, 256 * pair + 128 : 256 * pair + 256] = turned[64:128, :]
 
 
-def backward_body(own_ref, core_ref, cross_ref, wb_ref, slope_ref, image_ref, low_ref, rim_ref, pooled_ref, keep_ref, give_ref, pd, one):
-    for a, plane in enumerate(ordered(own_ref, core_ref, cross_ref)):
-        for (b, e), value in shifted(plane):
+def backward_body(delta_ref, wb_ref, slope_ref, image_ref, low_ref, rim_ref, pooled_ref, keep_ref, give_ref, pd, one):
+    for a in range(3):
+        for (b, e), value in shifted(delta_ref[128 * a : 128 * a + 128, :].astype(F32)):
             t = 26 - (a * 9 + b * 3 + e)
             pd[128 * t : 128 * t + 128, :] = value.astype(BF)
     back = mm(wb_ref[...], pd[...])
@@ -350,17 +384,21 @@
     k1 = jnp.transpose(kernel_one, (2, 3, 4, 1, 0)).reshape(864, 64)
     k2 = jnp.transpose(kernel_two, (2, 3, 4, 0, 1)).reshape(27, 8, 64)
     cot = cotangent.reshape(512, 64)
-    plane, row, corner = call(
-        edges_body,
-        [shape((512, 256), BF), shape((128, 256), BF), shape((32, 256), BF)],
-        [x],
-        [pltpu.VMEM((2, 1024, 128), F32)],
-    )
-    (packed,) = call(
+    plane, row, corner, packed = call(
         pack_body,
-        [shape((128, 1280), BF)],
-        [k2, cot, row],
-        [pltpu.VMEM((128, 1280), F32), pltpu.VMEM((512, 128), F32)],
+        [shape((512, 256), BF), shape((128, 256), BF), shape((32, 256), BF), shape((128, 1280), BF)],
+        [x, k2, cot],
+        [
+            pltpu.VMEM((2048, 256), BF),
+            pltpu.VMEM((27, 8, 64), BF),
+            pltpu.VMEM((512, 64), BF),
+            pltpu.VMEM((2, 1024, 128), F32),
+            pltpu.VMEM((128, 1280), F32),
+            pltpu.VMEM((512, 128), F32),
+            pltpu.SemaphoreType.DMA((3,)),
+        ],
+        space=pl.ANY,
+        limit=60 * 1024 * 1024,
     )
     plane = move(plane, "dev", 1)
     row = move(row, "ha", 1)
@@ -378,13 +416,11 @@
         [pltpu.VMEM((2048, 128), F32), pltpu.VMEM((2048, 128), F32)],
         flops=300000000,
     )
-    slope, pooled, one, other, low, top = call(
+    slope, pooled, low, top = call(
         first_layer_body,
         [
             shape((64, 2048), F32),
             shape((64, 256), BF),
-            shape((64, 128), BF),
-            shape((64, 128), BF),
             shape((16, 96, 128), BF),
             shape((5, 96, 128), BF),
         ],
@@ -392,13 +428,22 @@
         [pltpu.VMEM((672, 128), F32), pltpu.VMEM((672, 128), F32)],
         flops=400000000,
     )
-    w2, wb = call(turn_filters_body, [shape((128, 1792), BF), shape((64, 3456), BF)], [a2, swap(a2, "dev", 0)])
-    wide = jnp.concatenate([swap(one, "ha", 0), pooled, swap(other, "ha", 1)], axis=1)
+    other = swap(pooled, "dev", 0)
+    (rims,) = call(rims_body, [shape((128, 128), BF)], [pooled, other])
+    route = []
+    for d in range(n_dev):
+        for h in range(d % 2, n_ha - 1, 2):
+            route += [(d * n_ha + h, d * n_ha + h + 1), (d * n_ha + h + 1, d * n_ha + h)]
+    rims = lax.ppermute(rims, ("dev", "ha"), route)
+    a2_other = swap(a2, "dev", 0)
+    w2, wb = call(turn_filters_body, [shape((128, 1792), BF), shape((64, 3456), BF)], [a2, a2_other])
+    (pair,) = call(widen_body, [shape((128, 896), BF)], [pooled, other, rims, swap(rims, "dev", 0), a2])
+    cross = swap(pair, "dev", 1)
     patches, act, delta = call(
         second_layer_body,
-        [shape((1792, 384), BF), shape((128, 256), BF), shape((128, 384), BF)],
-        [wide, swap(wide, "dev", 0), swap(wide, "dev", 1), w2, a2],
-        flops=180000000,
+        [shape((2944, 384), BF), shape((128, 256), BF), shape((384, 384), BF)],
+        [pair, cross, swap(cross, "dev", 0), w2, a2_other],
+        flops=500000000,
     )
     keep_two, give_two = call(
         grad_two_body, [shape((128, 896), F32), shape((128, 896), BF)], [delta, patches], flops=180000000
@@ -406,7 +451,7 @@
     grad_pooled, keep_one, give_one = call(
         backward_body,
         [shape((64, 4, 64), BF), shape((128, 256), F32), shape((128, 256), BF)],
-        [delta, swap(delta, "dev", 0), swap(delta, "dev", 1), wb, slope, own, low, top],
+        [delta, wb, slope, own, low, top],
         [pltpu.VMEM((3456, 256), BF), pltpu.VMEM((2, 256, 128), F32)],
         flops=400000000,
     )

time: 108 us -> 105 us (0.972)
  blocking collectives: 51 us -> 43.6 us
  waiting for transfers between devices: 5.93 us -> 9.57 us
  Pallas kernels: 10.2 us -> 11.8 us
    all_to_all x3, blocking collectives: 51 us -> 43.6 us  [exchange(): lax.all_to_all(block, axis, 0, 0, tiled=True, axis_index_groups=groups)]
    ppermute x9 -> x7, waiting for transfers between devices: 5.92 us -> 9.56 us  [swap(): return lax.ppermute(block, axis, pairs + [(j, i) for i, j in pairs])]
    pallas_call x12 -> x13, Pallas kernels: 10.2 us -> 11.8 us  [call(): pl.pallas_call(body, out_shape=out_shape, in_specs=[pl.BlockSpec(memory_s...]
    unnamed x12 -> x4, local copies, waits for them, and re-layouts: 3.02 us -> 2.16 us
    ppermute x9 -> x7, starting transfers between devices: 12.1 us -> 11.5 us  [swap(): return lax.ppermute(block, axis, pairs + [(j, i) for i, j in pairs])]
  transfers between devices with their start and end apart: 13 -> 12, of which waited for: 4 -> 5; matrix products, arithmetic and copies ran while one was open for 0% -> 0% of each run, Pallas kernels for 5% -> 5%
where the time goes in v1:
time: 105 us
  blocking collectives  43.6 us (42%)
  starting transfers between devices  36.9 us (35%)
  Pallas kernels  11.8 us (11%)
  waiting for transfers between devices  9.57 us (9%)
  local copies, waits for them, and re-layouts  2.16 us (2%)
    all_to_all x3, blocking collectives, exchange(): lax.all_to_all(block, axis, 0, 0, tiled=True, axis_index_groups=groups)  43.6 us
    pallas_call x13, Pallas kernels, call(): pl.pallas_call(body, out_shape=out_shape, in_specs=[pl.BlockSpec(memory_s...  11.8 us
    all_to_all x1, starting transfers between devices, exchange(): lax.all_to_all(block, axis, 0, 0, tiled=True, axis_index_groups=groups)  11.6 us
    ppermute x7, starting transfers between devices, swap(): return lax.ppermute(block, axis, pairs + [(j, i) for i, j in pairs])  11.5 us
    ppermute x7, waiting for transfers between devices, swap(): return lax.ppermute(block, axis, pairs + [(j, i) for i, j in pairs])  9.56 us
    ppermute x2, starting transfers between devices, move(): lax.ppermute(block, axis, [(i, i + step) for i in range(size) if 0 <= i +...  7.93 us
    ppermute x1, starting transfers between devices, shards(): lax.ppermute(corner, ('dev', 'ha'), [(d * n_ha + h, (d + 1) * n_ha + h +...  5.21 us
    unnamed x4, local copies, waits for them, and re-layouts  2.16 us
  transfers between devices with their start and end apart: 12, of which 5 were waited for; matrix products, arithmetic and copies ran while one was open for 0% of the time, Pallas kernels for 5%

profile of v1, /device:TPU:1, one launch (start us, length us, event | category | flops | bytes accessed | tf_op | source)
XLA Modules:
  0.0 104.8 jit_solution(12499399654264219200)
XLA Ops:
  0.6 2.3 %shard_map.76 = (bf16[512,256]{1,0:T(8,128)(2,1)}, bf16[128,256]{1,0:T(8,128)(2,1)}, bf16[32,256]{1,0:T(8,128)(2,1)}, bf16[128,1280]{1,0:T(8,128)(2,1)}) custom-call(bf16[2048,256]{1,0:T(8,128)(2,1)} %bitcast.28, bf16[27,8,64]{2,1,0:T(8,128)(2,1)} %bitcast.42, bf16[512,64]{1,0:T(8,128)(2,1)} %bitcast.41), custom_call_target="tpu_custom_call" | custom-call | flops 1000000 | bytes 1813504 | tf_op jit(solution)/shard_map/pallas_call | solution.py:19
  2.9 11.6 %all-to-all-start = ((bf16[16,8,1280]{2,1,0:T(8,128)(2,1)}), bf16[16,8,1280]{2,1,0:T(8,128)(2,1)S(1)}, u32[]{:S(2)}, u32[]{:S(2)}) async-start(bf16[16,8,1280]{2,1,0:T(8,128)(2,1)} %bitcast.40), calls=%async_computation | async-start | bytes 655360 | tf_op jit(solution)/shard_map/all_to_all | solution.py:379
  14.5 3.5 %collective-permute-start = (bf16[512,256]{1,0:T(8,128)(2,1)}, bf16[512,256]{1,0:T(8,128)(2,1)S(1)}, u32[]{:S(2)}, u32[]{:S(2)}) collective-permute-start(bf16[512,256]{1,0:T(8,128)(2,1)} %get-tuple-element.30), channel_id=1, source_target_pairs={{0,16},{16,32},{32,48},{48,64},{64,80},{80,96},{96,112},{112,128},... | collective-permute-start | bytes 786440 | tf_op jit(solution)/shard_map/ppermute | solution.py:370
  18.0 4.4 %collective-permute-start.1 = (bf16[128,256]{1,0:T(8,128)(2,1)}, bf16[128,256]{1,0:T(8,128)(2,1)S(1)}, u32[]{:S(2)}, u32[]{:S(2)}) collective-permute-start(bf16[128,256]{1,0:T(8,128)(2,1)} %get-tuple-element.31), channel_id=1, source_target_pairs={{0,1},{1,2},{2,3},{3,4},{4,5},{5,6},{6,7},{7,8},{8,9},{9,10},{10,1... | collective-permute-start | bytes 196616 | tf_op jit(solution)/shard_map/ppermute | solution.py:370
  22.5 5.2 %collective-permute-start.2 = (bf16[32,256]{1,0:T(8,128)(2,1)}, bf16[32,256]{1,0:T(8,128)(2,1)S(1)}, u32[]{:S(2)}, u32[]{:S(2)}) collective-permute-start(bf16[32,256]{1,0:T(8,128)(2,1)} %get-tuple-element.32), channel_id=1, source_target_pairs={{0,17},{1,18},{2,19},{3,20},{4,21},{5,22},{6,23},{7,24},{8,25},{9,... | collective-permute-start | bytes 49160 | tf_op jit(solution)/shard_map/ppermute | solution.py:406
  27.7 1.2 %copy-done = bf16[32,4,16,256]{3,2,1,0:T(8,128)(2,1)S(1)} copy-done((bf16[32,4,16,256]{3,2,1,0:T(8,128)(2,1)S(1)}, bf16[32,4,16,256]{3,2,1,0:T(8,128)(2,1)}, u32[]{:S(2)}) %copy-start) | copy-done | bytes 1048600
  28.9 0.9 copy-done.1
  29.8 1.7 %shard_map.75 = (bf16[64,96,128]{2,1,0:T(8,128)(2,1)S(1)}, bf16[64,864]{1,0:T(8,128)(2,1)S(1)}) custom-call(bf16[2048,256]{1,0:T(8,128)(2,1)S(1)} %bitcast.29, bf16[864,64]{1,0:T(8,128)(2,1)S(1)} %bitcast.38), custom_call_target="tpu_custom_call" | custom-call | flops 300000000 | bytes 2842624 | tf_op jit(solution)/shard_map/pallas_call | solution.py:19
  31.6 1.4 %shard_map.77 = (f32[64,2048]{1,0:T(8,128)S(1)}, bf16[64,256]{1,0:T(8,128)(2,1)S(1)}, bf16[16,96,128]{2,1,0:T(8,128)(2,1)S(1)}, bf16[5,96,128]{2,1,0:T(8,128)(2,1)S(1)}) custom-call(bf16[64,96,128]{2,1,0:T(8,128)(2,1)S(1)} %get-tuple-element.28.own_ref.image_ref, bf16[64,864]{1,0:T(8,128)(2,1)S(1)} %get-tuple-element.29.wt_ref, ...), custom_call_target="tpu_custom_call" | custom-call | flops 400000000 | bytes 3100672 | tf_op jit(solution)/shard_map/pallas_call | solution.py:19
  33.4 0.9 collective-permute-done.3.other_ref
  34.3 0.7 collective-permute-start.4
  35.0 6.4 %collective-permute-start.5 = (bf16[128,128]{1,0:T(8,128)(2,1)S(1)}, bf16[128,128]{1,0:T(8,128)(2,1)S(1)}, u32[]{:S(2)}, u32[]{:S(2)}) collective-permute-start(bf16[128,128]{1,0:T(8,128)(2,1)S(1)} %collective-permute-done.4.mine_ref), channel_id=1, source_target_pairs={{0,16},{32,48},{64,80},{96,112},{128,144},{160,176},{192,208},{224... | collective-permute-start | bytes 98312 | tf_op jit(solution)/shard_map/ppermute | solution.py:375
  41.4 0.9 collective-permute-done.5.core_ref
  42.3 3.9 %collective-permute-start.6 = (bf16[128,896]{1,0:T(8,128)(2,1)S(1)}, bf16[128,896]{1,0:T(8,128)(2,1)S(1)}, u32[]{:S(2)}, u32[]{:S(2)}) collective-permute-start(bf16[128,896]{1,0:T(8,128)(2,1)S(1)} %shard_map.79.pair_ref), channel_id=1, source_target_pairs={{16,32},{48,64},{80,96},{112,128},{144,160},{176,192},{208,224},{3... | collective-permute-start | bytes 688136 | tf_op jit(solution)/shard_map/ppermute | solution.py:375
  46.2 5.7 %collective-permute-done.6.cross_ref = bf16[128,896]{1,0:T(8,128)(2,1)S(1)} collective-permute-done((bf16[128,896]{1,0:T(8,128)(2,1)S(1)}, bf16[128,896]{1,0:T(8,128)(2,1)S(1)}, u32[]{:S(2)}, u32[]{:S(2)}) %collective-permute-start.6) | collective-permute-done | bytes 229408 | tf_op jit(solution)/shard_map/ppermute | solution.py:375
  52.2 1.2 %collective-permute-done.7.core_ref = bf16[128,896]{1,0:T(8,128)(2,1)S(1)} collective-permute-done((bf16[128,896]{1,0:T(8,128)(2,1)S(1)}, bf16[128,896]{1,0:T(8,128)(2,1)S(1)}, u32[]{:S(2)}, u32[]{:S(2)}) %collective-permute-start.7) | collective-permute-done | bytes 229408 | tf_op jit(solution)/shard_map/ppermute | solution.py:375
  53.4 1.3 %shard_map.81 = (bf16[2944,384]{1,0:T(8,128)(2,1)S(1)}, bf16[128,256]{1,0:T(8,128)(2,1)S(1)}, bf16[384,384]{1,0:T(8,128)(2,1)S(1)}) custom-call(bf16[128,896]{1,0:T(8,128)(2,1)S(1)} %shard_map.79.pair_ref, bf16[128,896]{1,0:T(8,128)(2,1)S(1)} %collective-permute-done.6.cross_ref, bf16[128,896]{1,0:T(8,128)(2,1)S(1)} %collective-permute-done.7.core_ref, ...), custom_call_target="tpu_custom_call" | custom-call | flops 500000000 | bytes 4096000 | tf_op jit(solution)/shard_map/pallas_call | solution.py:19
  55.6 2.2 %shard_map.83 = (bf16[64,4,64]{2,1,0:T(4,128)(2,1)}, f32[128,256]{1,0:T(8,128)S(1)}, bf16[128,256]{1,0:T(8,128)(2,1)S(1)}) custom-call(bf16[384,384]{1,0:T(8,128)(2,1)S(1)} %get-tuple-element.36.delta_ref, bf16[64,3456]{1,0:T(8,128)(2,1)S(1)} %get-tuple-element.40.wb_ref, f32[64,2048]{1,0:T(8,128)S(1)} %get-tuple-element.41.slope_ref, ...), custom_call_target="tpu_custom_call" | custom-call | flops 400000000 | bytes 3579904 | tf_op jit(solution)/shard_map/pallas_call | solution.py:19
  58.3 0.9 collective-permute-done.10.other_one_ref
  59.2 12.4 %all_to_all.44 = bf16[8,16,1152]{2,1,0:T(8,128)(2,1)S(1)} all-to-all(bf16[8,16,1152]{2,1,0:T(8,128)(2,1)S(1)} %bitcast.34), channel_id=1, replica_groups={{0,32,64,96,128,160,192,224},{16,48,80,112,144,176,208,240},{1,33,65,97..., dimensions={0} | all-to-all | bytes 589824 | tf_op jit(solution)/shard_map/all_to_all | solution.py:379
  71.8 19.5 %all_to_all.45 = bf16[16,16,512]{2,1,0:T(8,128)(2,1)S(1)} all-to-all(bf16[16,16,512]{2,1,0:T(8,128)(2,1)S(1)} %bitcast.36), channel_id=1, replica_groups=mesh['dev'=16,'ha'=16] {'ha'}, dimensions={0} | all-to-all | bytes 524288 | tf_op jit(solution)/shard_map/all_to_all | solution.py:379
  91.2 0.9 shard_map.86
  92.1 11.7 %all_to_all.46 = bf16[16,16,384]{2,1,0:T(8,128)(2,1)S(1)} all-to-all(bf16[16,16,384]{2,1,0:T(8,128)(2,1)S(1)} %bitcast.39), channel_id=1, replica_groups=mesh['dev'=16,'ha'=16] {'dev'}, dimensions={0} | all-to-all | bytes 393216 | tf_op jit(solution)/shard_map/all_to_all | solution.py:379
  103.8 1.0 shard_map.87
  (20 shorter events, 2.3 us)
Async XLA Ops:
  2.9 39.3 %all-to-all-start = ((bf16[16,8,1280]{2,1,0:T(8,128)(2,1)}), bf16[16,8,1280]{2,1,0:T(8,128)(2,1)S(1)}, u32[]{:S(2)}, u32[]{:S(2)}) async-start(bf16[16,8,1280]{2,1,0:T(8,128)(2,1)} %bitcast.40), calls=%async_computation | async-start | bytes 655360 | tf_op jit(solution)/shard_map/all_to_all | solution.py:379
  14.5 17.1 %collective-permute-start = (bf16[512,256]{1,0:T(8,128)(2,1)}, bf16[512,256]{1,0:T(8,128)(2,1)S(1)}, u32[]{:S(2)}, u32[]{:S(2)}) collective-permute-start(bf16[512,256]{1,0:T(8,128)(2,1)} %get-tuple-element.30), channel_id=1, source_target_pairs={{0,16},{16,32},{32,48},{48,64},{64,80},{80,96},{96,112},{112,128},... | collective-permute-start | bytes 786440 | tf_op jit(solution)/shard_map/ppermute | solution.py:370
  18.0 13.5 %collective-permute-start.1 = (bf16[128,256]{1,0:T(8,128)(2,1)}, bf16[128,256]{1,0:T(8,128)(2,1)S(1)}, u32[]{:S(2)}, u32[]{:S(2)}) collective-permute-start(bf16[128,256]{1,0:T(8,128)(2,1)} %get-tuple-element.31), channel_id=1, source_target_pairs={{0,1},{1,2},{2,3},{3,4},{4,5},{5,6},{6,7},{7,8},{8,9},{9,10},{10,1... | collective-permute-start | bytes 196616 | tf_op jit(solution)/shard_map/ppermute | solution.py:370
  22.5 9.1 %collective-permute-start.2 = (bf16[32,256]{1,0:T(8,128)(2,1)}, bf16[32,256]{1,0:T(8,128)(2,1)S(1)}, u32[]{:S(2)}, u32[]{:S(2)}) collective-permute-start(bf16[32,256]{1,0:T(8,128)(2,1)} %get-tuple-element.32), channel_id=1, source_target_pairs={{0,17},{1,18},{2,19},{3,20},{4,21},{5,22},{6,23},{7,24},{8,25},{9,... | collective-permute-start | bytes 49160 | tf_op jit(solution)/shard_map/ppermute | solution.py:406
  27.7 1.2 %copy-start = (bf16[32,4,16,256]{3,2,1,0:T(8,128)(2,1)S(1)}, bf16[32,4,16,256]{3,2,1,0:T(8,128)(2,1)}, u32[]{:S(2)}) copy-start(bf16[32,4,16,256]{3,2,1,0:T(8,128)(2,1)} %param.4) | copy-start | bytes 3145732
  28.9 0.9 copy-start.1
  32.9 1.3 %collective-permute-start.3 = (bf16[64,256]{1,0:T(8,128)(2,1)S(1)}, bf16[64,256]{1,0:T(8,128)(2,1)S(1)}, u32[]{:S(2)}, u32[]{:S(2)}) collective-permute-start(bf16[64,256]{1,0:T(8,128)(2,1)S(1)} %get-tuple-element.33.own_ref), channel_id=1, source_target_pairs={{0,16},{32,48},{64,80},{96,112},{128,144},{160,176},{192,208},{224... | collective-permute-start | bytes 98312 | tf_op jit(solution)/shard_map/ppermute | solution.py:375
  34.3 0.7 collective-permute-start.4
  35.0 7.2 %collective-permute-start.5 = (bf16[128,128]{1,0:T(8,128)(2,1)S(1)}, bf16[128,128]{1,0:T(8,128)(2,1)S(1)}, u32[]{:S(2)}, u32[]{:S(2)}) collective-permute-start(bf16[128,128]{1,0:T(8,128)(2,1)S(1)} %collective-permute-done.4.mine_ref), channel_id=1, source_target_pairs={{0,16},{32,48},{64,80},{96,112},{128,144},{160,176},{192,208},{224... | collective-permute-start | bytes 98312 | tf_op jit(solution)/shard_map/ppermute | solution.py:375
  42.3 9.7 %collective-permute-start.6 = (bf16[128,896]{1,0:T(8,128)(2,1)S(1)}, bf16[128,896]{1,0:T(8,128)(2,1)S(1)}, u32[]{:S(2)}, u32[]{:S(2)}) collective-permute-start(bf16[128,896]{1,0:T(8,128)(2,1)S(1)} %shard_map.79.pair_ref), channel_id=1, source_target_pairs={{16,32},{48,64},{80,96},{112,128},{144,160},{176,192},{208,224},{3... | collective-permute-start | bytes 688136 | tf_op jit(solution)/shard_map/ppermute | solution.py:375
  46.1 5.8 %collective-permute-start.8 = (bf16[128,1280]{1,0:T(8,128)(2,1)S(1)}, bf16[128,1280]{1,0:T(8,128)(2,1)S(1)}, u32[]{:S(2)}, u32[]{:S(2)}) collective-permute-start(bf16[128,1280]{1,0:T(8,128)(2,1)S(1)} %bitcast.31), channel_id=1, source_target_pairs={{0,16},{32,48},{64,80},{96,112},{128,144},{160,176},{192,208},{224... | collective-permute-start | bytes 983048 | tf_op jit(solution)/shard_map/ppermute | solution.py:375
  51.9 1.5 %collective-permute-start.7 = (bf16[128,896]{1,0:T(8,128)(2,1)S(1)}, bf16[128,896]{1,0:T(8,128)(2,1)S(1)}, u32[]{:S(2)}, u32[]{:S(2)}) collective-permute-start(bf16[128,896]{1,0:T(8,128)(2,1)S(1)} %collective-permute-done.6.cross_ref), channel_id=1, source_target_pairs={{0,16},{32,48},{64,80},{96,112},{128,144},{160,176},{192,208},{224... | collective-permute-start | bytes 688136 | tf_op jit(solution)/shard_map/ppermute | solution.py:375
  55.4 3.8 %collective-permute-start.9 = (bf16[128,896]{1,0:T(8,128)(2,1)S(1)}, bf16[128,896]{1,0:T(8,128)(2,1)S(1)}, u32[]{:S(2)}, u32[]{:S(2)}) collective-permute-start(bf16[128,896]{1,0:T(8,128)(2,1)S(1)} %get-tuple-element.39), channel_id=1, source_target_pairs={{0,16},{32,48},{64,80},{96,112},{128,144},{160,176},{192,208},{224... | collective-permute-start | bytes 688136 | tf_op jit(solution)/shard_map/ppermute | solution.py:375
  57.8 1.4 %collective-permute-start.10 = (bf16[128,256]{1,0:T(8,128)(2,1)S(1)}, bf16[128,256]{1,0:T(8,128)(2,1)S(1)}, u32[]{:S(2)}, u32[]{:S(2)}) collective-permute-start(bf16[128,256]{1,0:T(8,128)(2,1)S(1)} %get-tuple-element.45), channel_id=1, source_target_pairs={{0,16},{32,48},{64,80},{96,112},{128,144},{160,176},{192,208},{224... | collective-permute-start | bytes 196616 | tf_op jit(solution)/shard_map/ppermute | solution.py:375

commit v2 on v1

--- a/solution.py
+++ b/solution.py
@@ -192,7 +192,7 @@
         out_ref[64 * k : 64 * k + 64, :] = jnp.where(bottom, value[:, 128:256], value[:, 0:128]).astype(BF)
 
 
-def widen_body(own_ref, other_ref, mine_ref, core_ref, a2_ref, out_ref):
+def widen_body(own_ref, other_ref, mine_ref, core_ref, out_ref):
     swapped = is_even("ha") == is_even("dev")
     mine, core = mine_ref[...].astype(F32), core_ref[...].astype(F32)
     for k, ref in enumerate((own_ref, other_ref)):
@@ -200,10 +200,9 @@
         out_ref[64 * k : 64 * k + 64, 0:128] = jnp.where(swapped, there, here).astype(BF)
         out_ref[64 * k : 64 * k + 64, 128:384] = ref[...]
         out_ref[64 * k : 64 * k + 64, 384:512] = jnp.where(swapped, here, there).astype(BF)
-    out_ref[:, 512:896] = a2_ref[:, 896:1280]
-
-
-def second_layer_body(pair_ref, cross_ref, core_ref, w2_ref, other_ref, patches_ref, act_ref, delta_ref):
+
+
+def second_layer_body(pair_ref, cross_ref, core_ref, w2_ref, a2_ref, other_ref, cot_ref, patches_ref, act_ref, delta_ref):
     even = is_even("dev")
 
     def planes(ref):
@@ -224,10 +223,10 @@
             t = a * 9 + b * 3 + e
             patches_ref[64 * t : 64 * t + 64, :] = value.astype(BF)
     patches_ref[2880:2944, :] = jnp.zeros((64, 384), BF)
-    cot_cross, cot_core = cross_ref[:, 512:896].astype(F32), other_ref[:, 896:1280].astype(F32)
+    cot_cross, cot_core = cot_ref[...].astype(F32), other_ref[:, 896:1280].astype(F32)
     cots = (
         jnp.where(even, cot_cross, cot_core),
-        pair_ref[:, 512:896].astype(F32),
+        a2_ref[:, 896:1280].astype(F32),
         jnp.where(even, cot_core, cot_cross),
     )
     for p in range(3):
@@ -329,24 +328,35 @@
         out_ref[16 * h : 16 * h + 16, 0:256] = one
 
 
-def sum_height_body(in_ref, act_ref, out_ref, acc):
+def sum_height_body(in_ref, out_ref):
     one, two = None, None
     for h in range(16):
         block = in_ref[16 * h : 16 * h + 16, :].astype(F32)
         one = block[:, 0:256] if h == 0 else one + block[:, 0:256]
         two = block[:, 384:512] if h == 0 else two + block[:, 384:512]
+    packed = jnp.concatenate([one, two], axis=1).astype(BF)
+    for c in range(8):
+        out_ref[16 * c : 16 * c + 16, :] = packed
+
+
+def lay_activation_body(in_ref, act_ref, acc):
+    for h in range(16):
+        block = in_ref[16 * h : 16 * h + 16, 256:384].astype(F32)
         for r in range(4):
-            value = block[8 * (r // 2) : 8 * (r // 2) + 8, 256:384]
+            value = block[8 * (r // 2) : 8 * (r // 2) + 8, :]
             acc[pl.ds(4 * h + r, 8, stride=64), :] = pltpu.roll(value, 64, 1) if r % 2 else value
     act_ref[...] = acc[...][:, 0:64].astype(BF)
-    packed = jnp.concatenate([one, two], axis=1).astype(BF)
-    for d in range(16):
-        out_ref[16 * d : 16 * d + 16, :] = packed
-
-
-def finish_body(in_ref, one_ref, two_ref, acc):
-    for part in range(3):
-        acc[part, :, :] = in_ref[:, 128 * part : 128 * part + 128].astype(F32)
+
+
+def finish_body(mine_ref, other_ref, one_ref, two_ref, acc):
+    even = is_even("dev")
+    for c in range(8):
+        mine = mine_ref[16 * c : 16 * c + 16, :].astype(F32)
+        other = other_ref[16 * c : 16 * c + 16, :].astype(F32)
+        first, second = jnp.where(even, mine, other), jnp.where(even, other, mine)
+        for part in range(3):
+            acc[part, 32 * c : 32 * c + 16, :] = first[:, 128 * part : 128 * part + 128]
+            acc[part, 32 * c + 16 : 32 * c + 32, :] = second[:, 128 * part : 128 * part + 128]
     for half in range(2):
         for m in range(7):
             value = acc[2, pl.ds(16 * half + m, 8, stride=32), :] * (1.0 / math.sqrt(CELLS_TWO))
@@ -437,12 +447,14 @@
     rims = lax.ppermute(rims, ("dev", "ha"), route)
     a2_other = swap(a2, "dev", 0)
     w2, wb = call(turn_filters_body, [shape((128, 1792), BF), shape((64, 3456), BF)], [a2, a2_other])
-    (pair,) = call(widen_body, [shape((128, 896), BF)], [pooled, other, rims, swap(rims, "dev", 0), a2])
+    cot_cross = swap(a2[:, 896:1280], "dev", 1)
+    rims_core, cot_cross = lax.optimization_barrier((swap(rims, "dev", 0), cot_cross))
+    (pair,) = call(widen_body, [shape((128, 512), BF)], [pooled, other, rims, rims_core])
     cross = swap(pair, "dev", 1)
     patches, act, delta = call(
         second_layer_body,
         [shape((2944, 384), BF), shape((128, 256), BF), shape((384, 384), BF)],
-        [pair, cross, swap(cross, "dev", 0), w2, a2_other],
+        [pair, cross, swap(cross, "dev", 0), w2, a2, a2_other, cot_cross],
         flops=500000000,
     )
     keep_two, give_two = call(
@@ -467,16 +479,14 @@
         [exchange(first, "dev", same_core), act],
         [pltpu.VMEM((2, 256, 128), F32)],
     )
-    activation, third = call(
-        sum_height_body,
-        [shape((512, 64), BF), shape((256, 384), BF)],
-        [exchange(second, "ha")],
-        [pltpu.VMEM((512, 128), F32)],
-    )
+    second = exchange(second, "ha")
+    (third,) = call(sum_height_body, [shape((128, 384), BF)], [second])
+    (activation,) = call(lay_activation_body, [shape((512, 64), BF)], [second], [pltpu.VMEM((512, 128), F32)])
+    third = exchange(third, "dev", same_core)
     one, two = call(
         finish_body,
         [shape((27, 32, 64), F32), shape((27, 8, 64), F32)],
-        [exchange(third, "dev")],
+        [third, swap(third, "dev", 0)],
         [pltpu.VMEM((3, 256, 128), F32)],
     )
     grad_one = jnp.transpose(one.reshape(3, 3, 3, 32, 64), (4, 3, 0, 1, 2))

time: 105 us -> 105 us (level)
  starting transfers between devices: 36.9 us -> 42.4 us
  waiting for transfers between devices: 9.57 us -> 5.62 us
  blocking collectives: 43.6 us -> 41.6 us
    ppermute x7 -> x9, starting transfers between devices: 11.5 us -> 17 us  [swap(): return lax.ppermute(block, axis, pairs + [(j, i) for i, j in pairs])]
    ppermute x7 -> x9, waiting for transfers between devices: 9.56 us -> 5.61 us  [swap(): return lax.ppermute(block, axis, pairs + [(j, i) for i, j in pairs])]
    all_to_all x3, blocking collectives: 43.6 us -> 41.6 us  [exchange(): lax.all_to_all(block, axis, 0, 0, tiled=True, axis_index_groups=groups)]
    pallas_call x13 -> x14, Pallas kernels: 11.8 us -> 11.8 us  [call(): pl.pallas_call(body, out_shape=out_shape, in_specs=[pl.BlockSpec(memory_s...]
  transfers between devices with their start and end apart: 12 -> 14, of which waited for: 5 -> 5; matrix products, arithmetic and copies ran while one was open for 0% -> 0% of each run, Pallas kernels for 5% -> 6%
where the time goes in v2:
time: 105 us
  starting transfers between devices  42.4 us (40%)
  blocking collectives  41.6 us (40%)
  Pallas kernels  11.8 us (11%)
  waiting for transfers between devices  5.62 us (5%)
  local copies, waits for them, and re-layouts  2.17 us (2%)
    all_to_all x3, blocking collectives, exchange(): lax.all_to_all(block, axis, 0, 0, tiled=True, axis_index_groups=groups)  41.6 us
    ppermute x9, starting transfers between devices, swap(): return lax.ppermute(block, axis, pairs + [(j, i) for i, j in pairs])  17 us
    pallas_call x14, Pallas kernels, call(): pl.pallas_call(body, out_shape=out_shape, in_specs=[pl.BlockSpec(memory_s...  11.8 us
    all_to_all x1, starting transfers between devices, exchange(): lax.all_to_all(block, axis, 0, 0, tiled=True, axis_index_groups=groups)  11.6 us
    ppermute x2, starting transfers between devices, move(): lax.ppermute(block, axis, [(i, i + step) for i in range(size) if 0 <= i +...  7.93 us
    ppermute x9, waiting for transfers between devices, swap(): return lax.ppermute(block, axis, pairs + [(j, i) for i, j in pairs])  5.61 us
    ppermute x1, starting transfers between devices, shards(): lax.ppermute(corner, ('dev', 'ha'), [(d * n_ha + h, (d + 1) * n_ha + h +...  5.21 us
    unnamed x4, local copies, waits for them, and re-layouts  2.16 us
  transfers between devices with their start and end apart: 14, of which 5 were waited for; matrix products, arithmetic and copies ran while one was open for 0% of the time, Pallas kernels for 6%

profile of v2, /device:TPU:1, one launch (start us, length us, event | category | flops | bytes accessed | tf_op | source)
XLA Modules:
  0.0 104.5 jit_solution(9925624470702145050)
XLA Ops:
  0.6 2.3 %shard_map.76 = (bf16[512,256]{1,0:T(8,128)(2,1)}, bf16[128,256]{1,0:T(8,128)(2,1)}, bf16[32,256]{1,0:T(8,128)(2,1)}, bf16[128,1280]{1,0:T(8,128)(2,1)}) custom-call(bf16[2048,256]{1,0:T(8,128)(2,1)} %bitcast.28, bf16[27,8,64]{2,1,0:T(8,128)(2,1)} %bitcast.46, bf16[512,64]{1,0:T(8,128)(2,1)} %bitcast.44), custom_call_target="tpu_custom_call" | custom-call | flops 1000000 | bytes 1813504 | tf_op jit(solution)/shard_map/pallas_call | solution.py:19
  2.9 11.6 %all-to-all-start = ((bf16[16,8,1280]{2,1,0:T(8,128)(2,1)}), bf16[16,8,1280]{2,1,0:T(8,128)(2,1)S(1)}, u32[]{:S(2)}, u32[]{:S(2)}) async-start(bf16[16,8,1280]{2,1,0:T(8,128)(2,1)} %bitcast.43), calls=%async_computation | async-start | bytes 655360 | tf_op jit(solution)/shard_map/all_to_all | solution.py:389
  14.5 3.5 %collective-permute-start = (bf16[512,256]{1,0:T(8,128)(2,1)}, bf16[512,256]{1,0:T(8,128)(2,1)S(1)}, u32[]{:S(2)}, u32[]{:S(2)}) collective-permute-start(bf16[512,256]{1,0:T(8,128)(2,1)} %get-tuple-element.30), channel_id=1, source_target_pairs={{0,16},{16,32},{32,48},{48,64},{64,80},{80,96},{96,112},{112,128},... | collective-permute-start | bytes 786440 | tf_op jit(solution)/shard_map/ppermute | solution.py:380
  18.0 4.4 %collective-permute-start.1 = (bf16[128,256]{1,0:T(8,128)(2,1)}, bf16[128,256]{1,0:T(8,128)(2,1)S(1)}, u32[]{:S(2)}, u32[]{:S(2)}) collective-permute-start(bf16[128,256]{1,0:T(8,128)(2,1)} %get-tuple-element.31), channel_id=1, source_target_pairs={{0,1},{1,2},{2,3},{3,4},{4,5},{5,6},{6,7},{7,8},{8,9},{9,10},{10,1... | collective-permute-start | bytes 196616 | tf_op jit(solution)/shard_map/ppermute | solution.py:380
  22.5 5.2 %collective-permute-start.2 = (bf16[32,256]{1,0:T(8,128)(2,1)}, bf16[32,256]{1,0:T(8,128)(2,1)S(1)}, u32[]{:S(2)}, u32[]{:S(2)}) collective-permute-start(bf16[32,256]{1,0:T(8,128)(2,1)} %get-tuple-element.32), channel_id=1, source_target_pairs={{0,17},{1,18},{2,19},{3,20},{4,21},{5,22},{6,23},{7,24},{8,25},{9,... | collective-permute-start | bytes 49160 | tf_op jit(solution)/shard_map/ppermute | solution.py:416
  27.7 1.2 %copy-done = bf16[32,4,16,256]{3,2,1,0:T(8,128)(2,1)S(1)} copy-done((bf16[32,4,16,256]{3,2,1,0:T(8,128)(2,1)S(1)}, bf16[32,4,16,256]{3,2,1,0:T(8,128)(2,1)}, u32[]{:S(2)}) %copy-start) | copy-done | bytes 1048600
  28.9 0.9 copy-done.1
  29.9 1.7 %shard_map.75 = (bf16[64,96,128]{2,1,0:T(8,128)(2,1)S(1)}, bf16[64,864]{1,0:T(8,128)(2,1)S(1)}) custom-call(bf16[2048,256]{1,0:T(8,128)(2,1)S(1)} %bitcast.29, bf16[864,64]{1,0:T(8,128)(2,1)S(1)} %bitcast.42), custom_call_target="tpu_custom_call" | custom-call | flops 300000000 | bytes 2842624 | tf_op jit(solution)/shard_map/pallas_call | solution.py:19
  31.6 1.4 %shard_map.77 = (f32[64,2048]{1,0:T(8,128)S(1)}, bf16[64,256]{1,0:T(8,128)(2,1)S(1)}, bf16[16,96,128]{2,1,0:T(8,128)(2,1)S(1)}, bf16[5,96,128]{2,1,0:T(8,128)(2,1)S(1)}) custom-call(bf16[64,96,128]{2,1,0:T(8,128)(2,1)S(1)} %get-tuple-element.28.own_ref.image_ref, bf16[64,864]{1,0:T(8,128)(2,1)S(1)} %get-tuple-element.29.wt_ref, ...), custom_call_target="tpu_custom_call" | custom-call | flops 400000000 | bytes 3100672 | tf_op jit(solution)/shard_map/pallas_call | solution.py:19
  33.5 3.6 %collective-permute-start.6 = (bf16[128,384]{1,0:T(8,128)(2,1)S(1)}, bf16[128,384]{1,0:T(8,128)(2,1)S(1)}, u32[]{:S(2)}, u32[]{:S(2)}) collective-permute-start(bf16[128,384]{1,0:T(8,128)(2,1)S(1)} %slice.4), channel_id=1, source_target_pairs={{16,32},{48,64},{80,96},{112,128},{144,160},{176,192},{208,224},{3... | collective-permute-start | bytes 294920 | tf_op jit(solution)/shard_map/ppermute | solution.py:385
  37.9 3.6 %collective-permute-start.5 = (bf16[128,128]{1,0:T(8,128)(2,1)S(1)}, bf16[128,128]{1,0:T(8,128)(2,1)S(1)}, u32[]{:S(2)}, u32[]{:S(2)}) collective-permute-start(bf16[128,128]{1,0:T(8,128)(2,1)S(1)} %collective-permute-done.4.mine_ref), channel_id=1, source_target_pairs={{0,16},{32,48},{64,80},{96,112},{128,144},{160,176},{192,208},{224... | collective-permute-start | bytes 98312 | tf_op jit(solution)/shard_map/ppermute | solution.py:385
  41.5 0.9 collective-permute-done.5.core_ref
  42.4 4.7 %collective-permute-start.7 = (bf16[128,512]{1,0:T(8,128)(2,1)S(1)}, bf16[128,512]{1,0:T(8,128)(2,1)S(1)}, u32[]{:S(2)}, u32[]{:S(2)}) collective-permute-start(bf16[128,512]{1,0:T(8,128)(2,1)S(1)} %shard_map.79.pair_ref), channel_id=1, source_target_pairs={{16,32},{48,64},{80,96},{112,128},{144,160},{176,192},{208,224},{3... | collective-permute-start | bytes 393224 | tf_op jit(solution)/shard_map/ppermute | solution.py:385
  47.0 2.6 %collective-permute-done.7.cross_ref = bf16[128,512]{1,0:T(8,128)(2,1)S(1)} collective-permute-done((bf16[128,512]{1,0:T(8,128)(2,1)S(1)}, bf16[128,512]{1,0:T(8,128)(2,1)S(1)}, u32[]{:S(2)}, u32[]{:S(2)}) %collective-permute-start.7) | collective-permute-done | bytes 131104 | tf_op jit(solution)/shard_map/ppermute | solution.py:385
  49.9 1.1 %collective-permute-done.8.core_ref = bf16[128,512]{1,0:T(8,128)(2,1)S(1)} collective-permute-done((bf16[128,512]{1,0:T(8,128)(2,1)S(1)}, bf16[128,512]{1,0:T(8,128)(2,1)S(1)}, u32[]{:S(2)}, u32[]{:S(2)}) %collective-permute-start.8) | collective-permute-done | bytes 131104 | tf_op jit(solution)/shard_map/ppermute | solution.py:385
  51.0 1.3 %shard_map.81 = (bf16[2944,384]{1,0:T(8,128)(2,1)S(1)}, bf16[128,256]{1,0:T(8,128)(2,1)S(1)}, bf16[384,384]{1,0:T(8,128)(2,1)S(1)}) custom-call(bf16[128,512]{1,0:T(8,128)(2,1)S(1)} %shard_map.79.pair_ref, bf16[128,512]{1,0:T(8,128)(2,1)S(1)} %collective-permute-done.7.cross_ref, bf16[128,512]{1,0:T(8,128)(2,1)S(1)} %collective-permute-done.8.core_ref, ...), custom_call_target="tpu_custom_call" | custom-call | flops 500000000 | bytes 4227072 | tf_op jit(solution)/shard_map/pallas_call | solution.py:19
  53.2 2.2 %shard_map.83 = (bf16[64,4,64]{2,1,0:T(4,128)(2,1)}, f32[128,256]{1,0:T(8,128)S(1)}, bf16[128,256]{1,0:T(8,128)(2,1)S(1)}) custom-call(bf16[384,384]{1,0:T(8,128)(2,1)S(1)} %get-tuple-element.38.delta_ref, bf16[64,3456]{1,0:T(8,128)(2,1)S(1)} %get-tuple-element.42.wb_ref, f32[64,2048]{1,0:T(8,128)S(1)} %get-tuple-element.43.slope_ref, ...), custom_call_target="tpu_custom_call" | custom-call | flops 400000000 | bytes 3579904 | tf_op jit(solution)/shard_map/pallas_call | solution.py:19
  55.9 0.9 collective-permute-done.11.other_one_ref
  56.8 15.0 %all_to_all.44 = bf16[8,16,1152]{2,1,0:T(8,128)(2,1)S(1)} all-to-all(bf16[8,16,1152]{2,1,0:T(8,128)(2,1)S(1)} %bitcast.37), channel_id=1, replica_groups={{0,32,64,96,128,160,192,224},{16,48,80,112,144,176,208,240},{1,33,65,97..., dimensions={0} | all-to-all | bytes 589824 | tf_op jit(solution)/shard_map/all_to_all | solution.py:389
  71.9 18.8 %all_to_all.45 = bf16[16,16,512]{2,1,0:T(8,128)(2,1)S(1)} all-to-all(bf16[16,16,512]{2,1,0:T(8,128)(2,1)S(1)} %bitcast.38), channel_id=1, replica_groups=mesh['dev'=16,'ha'=16] {'ha'}, dimensions={0} | all-to-all | bytes 524288 | tf_op jit(solution)/shard_map/all_to_all | solution.py:389
  90.7 7.9 %all_to_all.46 = bf16[8,16,384]{2,1,0:T(8,128)(2,1)S(1)} all-to-all(bf16[8,16,384]{2,1,0:T(8,128)(2,1)S(1)} %bitcast.41), channel_id=1, replica_groups={{0,32,64,96,128,160,192,224},{16,48,80,112,144,176,208,240},{1,33,65,97..., dimensions={0} | all-to-all | bytes 196608 | tf_op jit(solution)/shard_map/all_to_all | solution.py:389
  98.6 3.9 %collective-permute-start.12 = (bf16[128,384]{1,0:T(8,128)(2,1)S(1)}, bf16[128,384]{1,0:T(8,128)(2,1)S(1)}, u32[]{:S(2)}, u32[]{:S(2)}) collective-permute-start(bf16[128,384]{1,0:T(8,128)(2,1)S(1)} %bitcast.39), channel_id=1, source_target_pairs={{0,16},{32,48},{64,80},{96,112},{128,144},{160,176},{192,208},{224... | collective-permute-start | bytes 294920 | tf_op jit(solution)/shard_map/ppermute | solution.py:385
  102.5 0.8 shard_map.86
  103.5 1.0 shard_map.88
  (26 shorter events, 3.2 us)
Async XLA Ops:
  2.9 30.5 %all-to-all-start = ((bf16[16,8,1280]{2,1,0:T(8,128)(2,1)}), bf16[16,8,1280]{2,1,0:T(8,128)(2,1)S(1)}, u32[]{:S(2)}, u32[]{:S(2)}) async-start(bf16[16,8,1280]{2,1,0:T(8,128)(2,1)} %bitcast.43), calls=%async_computation | async-start | bytes 655360 | tf_op jit(solution)/shard_map/all_to_all | solution.py:389
  14.5 17.1 %collective-permute-start = (bf16[512,256]{1,0:T(8,128)(2,1)}, bf16[512,256]{1,0:T(8,128)(2,1)S(1)}, u32[]{:S(2)}, u32[]{:S(2)}) collective-permute-start(bf16[512,256]{1,0:T(8,128)(2,1)} %get-tuple-element.30), channel_id=1, source_target_pairs={{0,16},{16,32},{32,48},{48,64},{64,80},{80,96},{96,112},{112,128},... | collective-permute-start | bytes 786440 | tf_op jit(solution)/shard_map/ppermute | solution.py:380
  18.0 13.5 %collective-permute-start.1 = (bf16[128,256]{1,0:T(8,128)(2,1)}, bf16[128,256]{1,0:T(8,128)(2,1)S(1)}, u32[]{:S(2)}, u32[]{:S(2)}) collective-permute-start(bf16[128,256]{1,0:T(8,128)(2,1)} %get-tuple-element.31), channel_id=1, source_target_pairs={{0,1},{1,2},{2,3},{3,4},{4,5},{5,6},{6,7},{7,8},{8,9},{9,10},{10,1... | collective-permute-start | bytes 196616 | tf_op jit(solution)/shard_map/ppermute | solution.py:380
  22.5 9.1 %collective-permute-start.2 = (bf16[32,256]{1,0:T(8,128)(2,1)}, bf16[32,256]{1,0:T(8,128)(2,1)S(1)}, u32[]{:S(2)}, u32[]{:S(2)}) collective-permute-start(bf16[32,256]{1,0:T(8,128)(2,1)} %get-tuple-element.32), channel_id=1, source_target_pairs={{0,17},{1,18},{2,19},{3,20},{4,21},{5,22},{6,23},{7,24},{8,25},{9,... | collective-permute-start | bytes 49160 | tf_op jit(solution)/shard_map/ppermute | solution.py:416
  27.7 1.2 %copy-start = (bf16[32,4,16,256]{3,2,1,0:T(8,128)(2,1)S(1)}, bf16[32,4,16,256]{3,2,1,0:T(8,128)(2,1)}, u32[]{:S(2)}) copy-start(bf16[32,4,16,256]{3,2,1,0:T(8,128)(2,1)} %param.4) | copy-start | bytes 3145732
  28.9 0.9 copy-start.1
  33.0 4.1 %collective-permute-start.3 = (bf16[64,256]{1,0:T(8,128)(2,1)S(1)}, bf16[64,256]{1,0:T(8,128)(2,1)S(1)}, u32[]{:S(2)}, u32[]{:S(2)}) collective-permute-start(bf16[64,256]{1,0:T(8,128)(2,1)S(1)} %get-tuple-element.33.own_ref), channel_id=1, source_target_pairs={{0,16},{32,48},{64,80},{96,112},{128,144},{160,176},{192,208},{224... | collective-permute-start | bytes 98312 | tf_op jit(solution)/shard_map/ppermute | solution.py:385
  33.5 8.9 %collective-permute-start.6 = (bf16[128,384]{1,0:T(8,128)(2,1)S(1)}, bf16[128,384]{1,0:T(8,128)(2,1)S(1)}, u32[]{:S(2)}, u32[]{:S(2)}) collective-permute-start(bf16[128,384]{1,0:T(8,128)(2,1)S(1)} %slice.4), channel_id=1, source_target_pairs={{16,32},{48,64},{80,96},{112,128},{144,160},{176,192},{208,224},{3... | collective-permute-start | bytes 294920 | tf_op jit(solution)/shard_map/ppermute | solution.py:385
  37.1 0.8 collective-permute-start.4
  37.7 11.9 %collective-permute-start.9 = (bf16[128,1280]{1,0:T(8,128)(2,1)S(1)}, bf16[128,1280]{1,0:T(8,128)(2,1)S(1)}, u32[]{:S(2)}, u32[]{:S(2)}) collective-permute-start(bf16[128,1280]{1,0:T(8,128)(2,1)S(1)} %bitcast.33), channel_id=1, source_target_pairs={{0,16},{32,48},{64,80},{96,112},{128,144},{160,176},{192,208},{224... | collective-permute-start | bytes 983048 | tf_op jit(solution)/shard_map/ppermute | solution.py:385
  37.9 4.5 %collective-permute-start.5 = (bf16[128,128]{1,0:T(8,128)(2,1)S(1)}, bf16[128,128]{1,0:T(8,128)(2,1)S(1)}, u32[]{:S(2)}, u32[]{:S(2)}) collective-permute-start(bf16[128,128]{1,0:T(8,128)(2,1)S(1)} %collective-permute-done.4.mine_ref), channel_id=1, source_target_pairs={{0,16},{32,48},{64,80},{96,112},{128,144},{160,176},{192,208},{224... | collective-permute-start | bytes 98312 | tf_op jit(solution)/shard_map/ppermute | solution.py:385
  42.4 7.3 %collective-permute-start.7 = (bf16[128,512]{1,0:T(8,128)(2,1)S(1)}, bf16[128,512]{1,0:T(8,128)(2,1)S(1)}, u32[]{:S(2)}, u32[]{:S(2)}) collective-permute-start(bf16[128,512]{1,0:T(8,128)(2,1)S(1)} %shard_map.79.pair_ref), channel_id=1, source_target_pairs={{16,32},{48,64},{80,96},{112,128},{144,160},{176,192},{208,224},{3... | collective-permute-start | bytes 393224 | tf_op jit(solution)/shard_map/ppermute | solution.py:385
  49.7 1.3 %collective-permute-start.8 = (bf16[128,512]{1,0:T(8,128)(2,1)S(1)}, bf16[128,512]{1,0:T(8,128)(2,1)S(1)}, u32[]{:S(2)}, u32[]{:S(2)}) collective-permute-start(bf16[128,512]{1,0:T(8,128)(2,1)S(1)} %collective-permute-done.7.cross_ref), channel_id=1, source_target_pairs={{0,16},{32,48},{64,80},{96,112},{128,144},{160,176},{192,208},{224... | collective-permute-start | bytes 393224 | tf_op jit(solution)/shard_map/ppermute | solution.py:385
  53.0 3.8 %collective-permute-start.10 = (bf16[128,896]{1,0:T(8,128)(2,1)S(1)}, bf16[128,896]{1,0:T(8,128)(2,1)S(1)}, u32[]{:S(2)}, u32[]{:S(2)}) collective-permute-start(bf16[128,896]{1,0:T(8,128)(2,1)S(1)} %get-tuple-element.41), channel_id=1, source_target_pairs={{0,16},{32,48},{64,80},{96,112},{128,144},{160,176},{192,208},{224... | collective-permute-start | bytes 688136 | tf_op jit(solution)/shard_map/ppermute | solution.py:385
  55.4 1.3 %collective-permute-start.11 = (bf16[128,256]{1,0:T(8,128)(2,1)S(1)}, bf16[128,256]{1,0:T(8,128)(2,1)S(1)}, u32[]{:S(2)}, u32[]{:S(2)}) collective-permute-start(bf16[128,256]{1,0:T(8,128)(2,1)S(1)} %get-tuple-element.47), channel_id=1, source_target_pairs={{0,16},{32,48},{64,80},{96,112},{128,144},{160,176},{192,208},{224... | collective-permute-start | bytes 196616 | tf_op jit(solution)/shard_map/ppermute | solution.py:385
  98.6 4.9 %collective-permute-start.12 = (bf16[128,384]{1,0:T(8,128)(2,1)S(1)}, bf16[128,384]{1,0:T(8,128)(2,1)S(1)}, u32[]{:S(2)}, u32[]{:S(2)}) collective-permute-start(bf16[128,384]{1,0:T(8,128)(2,1)S(1)} %bitcast.39), channel_id=1, source_target_pairs={{0,16},{32,48},{64,80},{96,112},{128,144},{160,176},{192,208},{224... | collective-permute-start | bytes 294920 | tf_op jit(solution)/shard_map/ppermute | solution.py:385

commit v3 on v2

--- a/solution.py
+++ b/solution.py
@@ -75,7 +75,7 @@
     for h in range(16):
         acc[8 * h : 8 * h + 8, 0:896] = filters
     copies[2].wait()
-    cots[...] = jnp.concatenate([cot_ref[...].astype(F32), jnp.zeros((512, 64), F32)], axis=1)
+    cots[0:512, :] = jnp.concatenate([cot_ref[...].astype(F32), jnp.zeros((512, 64), F32)], axis=1)
     for h in range(16):
         for part in range(3):
             two = []
@@ -321,8 +321,8 @@
         for side in range(2):
             at = 16 * h + 8 * side
             acc[0, at : at + 8, :] = act[8 * h : 8 * h + 8, 128 * side : 128 * side + 128]
-    out_ref[:, 256:384] = acc[0].astype(BF)
-    out_ref[:, 384:512] = acc[1].astype(BF)
+    out_ref[:, 256:384] = acc[0, 0:256, :].astype(BF)
+    out_ref[:, 384:512] = acc[1, 0:256, :].astype(BF)
     one = total[:, 896:1152].astype(BF)
     for h in range(16):
         out_ref[16 * h : 16 * h + 16, 0:256] = one
@@ -345,7 +345,7 @@
         for r in range(4):
             value = block[8 * (r // 2) : 8 * (r // 2) + 8, :]
             acc[pl.ds(4 * h + r, 8, stride=64), :] = pltpu.roll(value, 64, 1) if r % 2 else value
-    act_ref[...] = acc[...][:, 0:64].astype(BF)
+    act_ref[...] = acc[0:512, :][:, 0:64].astype(BF)
 
 
 def finish_body(mine_ref, other_ref, one_ref, two_ref, acc):
@@ -402,9 +402,9 @@
             pltpu.VMEM((2048, 256), BF),
             pltpu.VMEM((27, 8, 64), BF),
             pltpu.VMEM((512, 64), BF),
-            pltpu.VMEM((2, 1024, 128), F32),
+            pltpu.VMEM((2, 1056, 128), F32),
             pltpu.VMEM((128, 1280), F32),
-            pltpu.VMEM((512, 128), F32),
+            pltpu.VMEM((576, 128), F32),
             pltpu.SemaphoreType.DMA((3,)),
         ],
         space=pl.ANY,
@@ -423,7 +423,7 @@
         turn_image_body,
         [shape((64, 96, 128), BF), shape((64, 864), BF)],
         [x, k1],
-        [pltpu.VMEM((2048, 128), F32), pltpu.VMEM((2048, 128), F32)],
+        [pltpu.VMEM((2112, 128), F32), pltpu.VMEM((2112, 128), F32)],
         flops=300000000,
     )
     slope, pooled, low, top = call(
@@ -464,7 +464,7 @@
         backward_body,
         [shape((64, 4, 64), BF), shape((128, 256), F32), shape((128, 256), BF)],
         [delta, wb, slope, own, low, top],
-        [pltpu.VMEM((3456, 256), BF), pltpu.VMEM((2, 256, 128), F32)],
+        [pltpu.VMEM((3456, 256), BF), pltpu.VMEM((2, 272, 128), F32)],
         flops=400000000,
     )
     (first,) = call(
@@ -477,17 +477,17 @@
         sum_depth_body,
         [shape((256, 512), BF)],
         [exchange(first, "dev", same_core), act],
-        [pltpu.VMEM((2, 256, 128), F32)],
+        [pltpu.VMEM((2, 272, 128), F32)],
     )
     second = exchange(second, "ha")
     (third,) = call(sum_height_body, [shape((128, 384), BF)], [second])
-    (activation,) = call(lay_activation_body, [shape((512, 64), BF)], [second], [pltpu.VMEM((512, 128), F32)])
+    (activation,) = call(lay_activation_body, [shape((512, 64), BF)], [second], [pltpu.VMEM((576, 128), F32)])
     third = exchange(third, "dev", same_core)
     one, two = call(
         finish_body,
         [shape((27, 32, 64), F32), shape((27, 8, 64), F32)],
         [third, swap(third, "dev", 0)],
-        [pltpu.VMEM((3, 256, 128), F32)],
+        [pltpu.VMEM((3, 288, 128), F32)],
     )
     grad_one = jnp.transpose(one.reshape(3, 3, 3, 32, 64), (4, 3, 0, 1, 2))
     grad_two = jnp.transpose(two.reshape(3, 3, 3, 8, 64), (3, 4, 0, 1, 2))

time: 105 us -> 105 us (level)
  no operation moved by 1% of the time
where the time goes in v3:
time: 105 us
  starting transfers between devices  42.4 us (40%)
  blocking collectives  41.6 us (40%)
  Pallas kernels  11.8 us (11%)
  waiting for transfers between devices  5.62 us (5%)
  local copies, waits for them, and re-layouts  2.17 us (2%)
    all_to_all x3, blocking collectives, exchange(): lax.all_to_all(block, axis, 0, 0, tiled=True, axis_index_groups=groups)  41.6 us
    ppermute x9, starting transfers between devices, swap(): return lax.ppermute(block, axis, pairs + [(j, i) for i, j in pairs])  17 us
    pallas_call x14, Pallas kernels, call(): pl.pallas_call(body, out_shape=out_shape, in_specs=[pl.BlockSpec(memory_s...  11.8 us
    all_to_all x1, starting transfers between devices, exchange(): lax.all_to_all(block, axis, 0, 0, tiled=True, axis_index_groups=groups)  11.6 us
    ppermute x2, starting transfers between devices, move(): lax.ppermute(block, axis, [(i, i + step) for i in range(size) if 0 <= i +...  7.93 us
    ppermute x9, waiting for transfers between devices, swap(): return lax.ppermute(block, axis, pairs + [(j, i) for i, j in pairs])  5.61 us
    ppermute x1, starting transfers between devices, shards(): lax.ppermute(corner, ('dev', 'ha'), [(d * n_ha + h, (d + 1) * n_ha + h +...  5.21 us
    unnamed x4, local copies, waits for them, and re-layouts  2.16 us
  transfers between devices with their start and end apart: 14, of which 5 were waited for; matrix products, arithmetic and copies ran while one was open for 0% of the time, Pallas kernels for 6%

profile of v3, /device:TPU:1, one launch (start us, length us, event | category | flops | bytes accessed | tf_op | source)
XLA Modules:
  0.0 104.5 jit_solution(15595776231654081637)
XLA Ops:
  0.6 2.3 %shard_map.76 = (bf16[512,256]{1,0:T(8,128)(2,1)}, bf16[128,256]{1,0:T(8,128)(2,1)}, bf16[32,256]{1,0:T(8,128)(2,1)}, bf16[128,1280]{1,0:T(8,128)(2,1)}) custom-call(bf16[2048,256]{1,0:T(8,128)(2,1)} %bitcast.28, bf16[27,8,64]{2,1,0:T(8,128)(2,1)} %bitcast.46, bf16[512,64]{1,0:T(8,128)(2,1)} %bitcast.44), custom_call_target="tpu_custom_call" | custom-call | flops 1000000 | bytes 1813504 | tf_op jit(solution)/shard_map/pallas_call | solution.py:19
  2.9 11.6 %all-to-all-start = ((bf16[16,8,1280]{2,1,0:T(8,128)(2,1)}), bf16[16,8,1280]{2,1,0:T(8,128)(2,1)S(1)}, u32[]{:S(2)}, u32[]{:S(2)}) async-start(bf16[16,8,1280]{2,1,0:T(8,128)(2,1)} %bitcast.43), calls=%async_computation | async-start | bytes 655360 | tf_op jit(solution)/shard_map/all_to_all | solution.py:389
  14.5 3.5 %collective-permute-start = (bf16[512,256]{1,0:T(8,128)(2,1)}, bf16[512,256]{1,0:T(8,128)(2,1)S(1)}, u32[]{:S(2)}, u32[]{:S(2)}) collective-permute-start(bf16[512,256]{1,0:T(8,128)(2,1)} %get-tuple-element.30), channel_id=1, source_target_pairs={{0,16},{16,32},{32,48},{48,64},{64,80},{80,96},{96,112},{112,128},... | collective-permute-start | bytes 786440 | tf_op jit(solution)/shard_map/ppermute | solution.py:380
  18.0 4.4 %collective-permute-start.1 = (bf16[128,256]{1,0:T(8,128)(2,1)}, bf16[128,256]{1,0:T(8,128)(2,1)S(1)}, u32[]{:S(2)}, u32[]{:S(2)}) collective-permute-start(bf16[128,256]{1,0:T(8,128)(2,1)} %get-tuple-element.31), channel_id=1, source_target_pairs={{0,1},{1,2},{2,3},{3,4},{4,5},{5,6},{6,7},{7,8},{8,9},{9,10},{10,1... | collective-permute-start | bytes 196616 | tf_op jit(solution)/shard_map/ppermute | solution.py:380
  22.5 5.2 %collective-permute-start.2 = (bf16[32,256]{1,0:T(8,128)(2,1)}, bf16[32,256]{1,0:T(8,128)(2,1)S(1)}, u32[]{:S(2)}, u32[]{:S(2)}) collective-permute-start(bf16[32,256]{1,0:T(8,128)(2,1)} %get-tuple-element.32), channel_id=1, source_target_pairs={{0,17},{1,18},{2,19},{3,20},{4,21},{5,22},{6,23},{7,24},{8,25},{9,... | collective-permute-start | bytes 49160 | tf_op jit(solution)/shard_map/ppermute | solution.py:416
  27.7 1.2 %copy-done = bf16[32,4,16,256]{3,2,1,0:T(8,128)(2,1)S(1)} copy-done((bf16[32,4,16,256]{3,2,1,0:T(8,128)(2,1)S(1)}, bf16[32,4,16,256]{3,2,1,0:T(8,128)(2,1)}, u32[]{:S(2)}) %copy-start) | copy-done | bytes 1048600
  28.9 0.9 copy-done.1
  29.9 1.7 %shard_map.75 = (bf16[64,96,128]{2,1,0:T(8,128)(2,1)S(1)}, bf16[64,864]{1,0:T(8,128)(2,1)S(1)}) custom-call(bf16[2048,256]{1,0:T(8,128)(2,1)S(1)} %bitcast.29, bf16[864,64]{1,0:T(8,128)(2,1)S(1)} %bitcast.42), custom_call_target="tpu_custom_call" | custom-call | flops 300000000 | bytes 2842624 | tf_op jit(solution)/shard_map/pallas_call | solution.py:19
  31.6 1.4 %shard_map.77 = (f32[64,2048]{1,0:T(8,128)S(1)}, bf16[64,256]{1,0:T(8,128)(2,1)S(1)}, bf16[16,96,128]{2,1,0:T(8,128)(2,1)S(1)}, bf16[5,96,128]{2,1,0:T(8,128)(2,1)S(1)}) custom-call(bf16[64,96,128]{2,1,0:T(8,128)(2,1)S(1)} %get-tuple-element.28.own_ref.image_ref, bf16[64,864]{1,0:T(8,128)(2,1)S(1)} %get-tuple-element.29.wt_ref, ...), custom_call_target="tpu_custom_call" | custom-call | flops 400000000 | bytes 3100672 | tf_op jit(solution)/shard_map/pallas_call | solution.py:19
  33.5 3.6 %collective-permute-start.6 = (bf16[128,384]{1,0:T(8,128)(2,1)S(1)}, bf16[128,384]{1,0:T(8,128)(2,1)S(1)}, u32[]{:S(2)}, u32[]{:S(2)}) collective-permute-start(bf16[128,384]{1,0:T(8,128)(2,1)S(1)} %slice.4), channel_id=1, source_target_pairs={{16,32},{48,64},{80,96},{112,128},{144,160},{176,192},{208,224},{3... | collective-permute-start | bytes 294920 | tf_op jit(solution)/shard_map/ppermute | solution.py:385
  37.9 3.6 %collective-permute-start.5 = (bf16[128,128]{1,0:T(8,128)(2,1)S(1)}, bf16[128,128]{1,0:T(8,128)(2,1)S(1)}, u32[]{:S(2)}, u32[]{:S(2)}) collective-permute-start(bf16[128,128]{1,0:T(8,128)(2,1)S(1)} %collective-permute-done.4.mine_ref), channel_id=1, source_target_pairs={{0,16},{32,48},{64,80},{96,112},{128,144},{160,176},{192,208},{224... | collective-permute-start | bytes 98312 | tf_op jit(solution)/shard_map/ppermute | solution.py:385
  41.5 0.9 collective-permute-done.5.core_ref
  42.4 4.7 %collective-permute-start.7 = (bf16[128,512]{1,0:T(8,128)(2,1)S(1)}, bf16[128,512]{1,0:T(8,128)(2,1)S(1)}, u32[]{:S(2)}, u32[]{:S(2)}) collective-permute-start(bf16[128,512]{1,0:T(8,128)(2,1)S(1)} %shard_map.79.pair_ref), channel_id=1, source_target_pairs={{16,32},{48,64},{80,96},{112,128},{144,160},{176,192},{208,224},{3... | collective-permute-start | bytes 393224 | tf_op jit(solution)/shard_map/ppermute | solution.py:385
  47.0 2.6 %collective-permute-done.7.cross_ref = bf16[128,512]{1,0:T(8,128)(2,1)S(1)} collective-permute-done((bf16[128,512]{1,0:T(8,128)(2,1)S(1)}, bf16[128,512]{1,0:T(8,128)(2,1)S(1)}, u32[]{:S(2)}, u32[]{:S(2)}) %collective-permute-start.7) | collective-permute-done | bytes 131104 | tf_op jit(solution)/shard_map/ppermute | solution.py:385
  49.9 1.1 %collective-permute-done.8.core_ref = bf16[128,512]{1,0:T(8,128)(2,1)S(1)} collective-permute-done((bf16[128,512]{1,0:T(8,128)(2,1)S(1)}, bf16[128,512]{1,0:T(8,128)(2,1)S(1)}, u32[]{:S(2)}, u32[]{:S(2)}) %collective-permute-start.8) | collective-permute-done | bytes 131104 | tf_op jit(solution)/shard_map/ppermute | solution.py:385
  51.0 1.3 %shard_map.81 = (bf16[2944,384]{1,0:T(8,128)(2,1)S(1)}, bf16[128,256]{1,0:T(8,128)(2,1)S(1)}, bf16[384,384]{1,0:T(8,128)(2,1)S(1)}) custom-call(bf16[128,512]{1,0:T(8,128)(2,1)S(1)} %shard_map.79.pair_ref, bf16[128,512]{1,0:T(8,128)(2,1)S(1)} %collective-permute-done.7.cross_ref, bf16[128,512]{1,0:T(8,128)(2,1)S(1)} %collective-permute-done.8.core_ref, ...), custom_call_target="tpu_custom_call" | custom-call | flops 500000000 | bytes 4227072 | tf_op jit(solution)/shard_map/pallas_call | solution.py:19
  53.2 2.2 %shard_map.83 = (bf16[64,4,64]{2,1,0:T(4,128)(2,1)}, f32[128,256]{1,0:T(8,128)S(1)}, bf16[128,256]{1,0:T(8,128)(2,1)S(1)}) custom-call(bf16[384,384]{1,0:T(8,128)(2,1)S(1)} %get-tuple-element.38.delta_ref, bf16[64,3456]{1,0:T(8,128)(2,1)S(1)} %get-tuple-element.42.wb_ref, f32[64,2048]{1,0:T(8,128)S(1)} %get-tuple-element.43.slope_ref, ...), custom_call_target="tpu_custom_call" | custom-call | flops 400000000 | bytes 3579904 | tf_op jit(solution)/shard_map/pallas_call | solution.py:19
  55.9 0.9 collective-permute-done.11.other_one_ref
  56.8 15.0 %all_to_all.44 = bf16[8,16,1152]{2,1,0:T(8,128)(2,1)S(1)} all-to-all(bf16[8,16,1152]{2,1,0:T(8,128)(2,1)S(1)} %bitcast.37), channel_id=1, replica_groups={{0,32,64,96,128,160,192,224},{16,48,80,112,144,176,208,240},{1,33,65,97..., dimensions={0} | all-to-all | bytes 589824 | tf_op jit(solution)/shard_map/all_to_all | solution.py:389
  71.9 18.8 %all_to_all.45 = bf16[16,16,512]{2,1,0:T(8,128)(2,1)S(1)} all-to-all(bf16[16,16,512]{2,1,0:T(8,128)(2,1)S(1)} %bitcast.38), channel_id=1, replica_groups=mesh['dev'=16,'ha'=16] {'ha'}, dimensions={0} | all-to-all | bytes 524288 | tf_op jit(solution)/shard_map/all_to_all | solution.py:389
  90.7 7.9 %all_to_all.46 = bf16[8,16,384]{2,1,0:T(8,128)(2,1)S(1)} all-to-all(bf16[8,16,384]{2,1,0:T(8,128)(2,1)S(1)} %bitcast.41), channel_id=1, replica_groups={{0,32,64,96,128,160,192,224},{16,48,80,112,144,176,208,240},{1,33,65,97..., dimensions={0} | all-to-all | bytes 196608 | tf_op jit(solution)/shard_map/all_to_all | solution.py:389
  98.6 3.9 %collective-permute-start.12 = (bf16[128,384]{1,0:T(8,128)(2,1)S(1)}, bf16[128,384]{1,0:T(8,128)(2,1)S(1)}, u32[]{:S(2)}, u32[]{:S(2)}) collective-permute-start(bf16[128,384]{1,0:T(8,128)(2,1)S(1)} %bitcast.39), channel_id=1, source_target_pairs={{0,16},{32,48},{64,80},{96,112},{128,144},{160,176},{192,208},{224... | collective-permute-start | bytes 294920 | tf_op jit(solution)/shard_map/ppermute | solution.py:385
  102.5 0.8 shard_map.86
  103.5 1.0 shard_map.88
  (26 shorter events, 3.2 us)
Async XLA Ops:
  2.9 30.5 %all-to-all-start = ((bf16[16,8,1280]{2,1,0:T(8,128)(2,1)}), bf16[16,8,1280]{2,1,0:T(8,128)(2,1)S(1)}, u32[]{:S(2)}, u32[]{:S(2)}) async-start(bf16[16,8,1280]{2,1,0:T(8,128)(2,1)} %bitcast.43), calls=%async_computation | async-start | bytes 655360 | tf_op jit(solution)/shard_map/all_to_all | solution.py:389
  14.5 17.1 %collective-permute-start = (bf16[512,256]{1,0:T(8,128)(2,1)}, bf16[512,256]{1,0:T(8,128)(2,1)S(1)}, u32[]{:S(2)}, u32[]{:S(2)}) collective-permute-start(bf16[512,256]{1,0:T(8,128)(2,1)} %get-tuple-element.30), channel_id=1, source_target_pairs={{0,16},{16,32},{32,48},{48,64},{64,80},{80,96},{96,112},{112,128},... | collective-permute-start | bytes 786440 | tf_op jit(solution)/shard_map/ppermute | solution.py:380
  18.0 13.5 %collective-permute-start.1 = (bf16[128,256]{1,0:T(8,128)(2,1)}, bf16[128,256]{1,0:T(8,128)(2,1)S(1)}, u32[]{:S(2)}, u32[]{:S(2)}) collective-permute-start(bf16[128,256]{1,0:T(8,128)(2,1)} %get-tuple-element.31), channel_id=1, source_target_pairs={{0,1},{1,2},{2,3},{3,4},{4,5},{5,6},{6,7},{7,8},{8,9},{9,10},{10,1... | collective-permute-start | bytes 196616 | tf_op jit(solution)/shard_map/ppermute | solution.py:380
  22.5 9.1 %collective-permute-start.2 = (bf16[32,256]{1,0:T(8,128)(2,1)}, bf16[32,256]{1,0:T(8,128)(2,1)S(1)}, u32[]{:S(2)}, u32[]{:S(2)}) collective-permute-start(bf16[32,256]{1,0:T(8,128)(2,1)} %get-tuple-element.32), channel_id=1, source_target_pairs={{0,17},{1,18},{2,19},{3,20},{4,21},{5,22},{6,23},{7,24},{8,25},{9,... | collective-permute-start | bytes 49160 | tf_op jit(solution)/shard_map/ppermute | solution.py:416
  27.7 1.2 %copy-start = (bf16[32,4,16,256]{3,2,1,0:T(8,128)(2,1)S(1)}, bf16[32,4,16,256]{3,2,1,0:T(8,128)(2,1)}, u32[]{:S(2)}) copy-start(bf16[32,4,16,256]{3,2,1,0:T(8,128)(2,1)} %param.4) | copy-start | bytes 3145732
  28.9 0.9 copy-start.1
  33.0 4.1 %collective-permute-start.3 = (bf16[64,256]{1,0:T(8,128)(2,1)S(1)}, bf16[64,256]{1,0:T(8,128)(2,1)S(1)}, u32[]{:S(2)}, u32[]{:S(2)}) collective-permute-start(bf16[64,256]{1,0:T(8,128)(2,1)S(1)} %get-tuple-element.33.own_ref), channel_id=1, source_target_pairs={{0,16},{32,48},{64,80},{96,112},{128,144},{160,176},{192,208},{224... | collective-permute-start | bytes 98312 | tf_op jit(solution)/shard_map/ppermute | solution.py:385
  33.5 8.9 %collective-permute-start.6 = (bf16[128,384]{1,0:T(8,128)(2,1)S(1)}, bf16[128,384]{1,0:T(8,128)(2,1)S(1)}, u32[]{:S(2)}, u32[]{:S(2)}) collective-permute-start(bf16[128,384]{1,0:T(8,128)(2,1)S(1)} %slice.4), channel_id=1, source_target_pairs={{16,32},{48,64},{80,96},{112,128},{144,160},{176,192},{208,224},{3... | collective-permute-start | bytes 294920 | tf_op jit(solution)/shard_map/ppermute | solution.py:385
  37.1 0.8 collective-permute-start.4
  37.7 11.9 %collective-permute-start.9 = (bf16[128,1280]{1,0:T(8,128)(2,1)S(1)}, bf16[128,1280]{1,0:T(8,128)(2,1)S(1)}, u32[]{:S(2)}, u32[]{:S(2)}) collective-permute-start(bf16[128,1280]{1,0:T(8,128)(2,1)S(1)} %bitcast.33), channel_id=1, source_target_pairs={{0,16},{32,48},{64,80},{96,112},{128,144},{160,176},{192,208},{224... | collective-permute-start | bytes 983048 | tf_op jit(solution)/shard_map/ppermute | solution.py:385
  37.9 4.5 %collective-permute-start.5 = (bf16[128,128]{1,0:T(8,128)(2,1)S(1)}, bf16[128,128]{1,0:T(8,128)(2,1)S(1)}, u32[]{:S(2)}, u32[]{:S(2)}) collective-permute-start(bf16[128,128]{1,0:T(8,128)(2,1)S(1)} %collective-permute-done.4.mine_ref), channel_id=1, source_target_pairs={{0,16},{32,48},{64,80},{96,112},{128,144},{160,176},{192,208},{224... | collective-permute-start | bytes 98312 | tf_op jit(solution)/shard_map/ppermute | solution.py:385
  42.4 7.3 %collective-permute-start.7 = (bf16[128,512]{1,0:T(8,128)(2,1)S(1)}, bf16[128,512]{1,0:T(8,128)(2,1)S(1)}, u32[]{:S(2)}, u32[]{:S(2)}) collective-permute-start(bf16[128,512]{1,0:T(8,128)(2,1)S(1)} %shard_map.79.pair_ref), channel_id=1, source_target_pairs={{16,32},{48,64},{80,96},{112,128},{144,160},{176,192},{208,224},{3... | collective-permute-start | bytes 393224 | tf_op jit(solution)/shard_map/ppermute | solution.py:385
  49.7 1.3 %collective-permute-start.8 = (bf16[128,512]{1,0:T(8,128)(2,1)S(1)}, bf16[128,512]{1,0:T(8,128)(2,1)S(1)}, u32[]{:S(2)}, u32[]{:S(2)}) collective-permute-start(bf16[128,512]{1,0:T(8,128)(2,1)S(1)} %collective-permute-done.7.cross_ref), channel_id=1, source_target_pairs={{0,16},{32,48},{64,80},{96,112},{128,144},{160,176},{192,208},{224... | collective-permute-start | bytes 393224 | tf_op jit(solution)/shard_map/ppermute | solution.py:385
  53.0 3.8 %collective-permute-start.10 = (bf16[128,896]{1,0:T(8,128)(2,1)S(1)}, bf16[128,896]{1,0:T(8,128)(2,1)S(1)}, u32[]{:S(2)}, u32[]{:S(2)}) collective-permute-start(bf16[128,896]{1,0:T(8,128)(2,1)S(1)} %get-tuple-element.41), channel_id=1, source_target_pairs={{0,16},{32,48},{64,80},{96,112},{128,144},{160,176},{192,208},{224... | collective-permute-start | bytes 688136 | tf_op jit(solution)/shard_map/ppermute | solution.py:385
  55.4 1.3 %collective-permute-start.11 = (bf16[128,256]{1,0:T(8,128)(2,1)S(1)}, bf16[128,256]{1,0:T(8,128)(2,1)S(1)}, u32[]{:S(2)}, u32[]{:S(2)}) collective-permute-start(bf16[128,256]{1,0:T(8,128)(2,1)S(1)} %get-tuple-element.47), channel_id=1, source_target_pairs={{0,16},{32,48},{64,80},{96,112},{128,144},{160,176},{192,208},{224... | collective-permute-start | bytes 196616 | tf_op jit(solution)/shard_map/ppermute | solution.py:385
  98.6 4.9 %collective-permute-start.12 = (bf16[128,384]{1,0:T(8,128)(2,1)S(1)}, bf16[128,384]{1,0:T(8,128)(2,1)S(1)}, u32[]{:S(2)}, u32[]{:S(2)}) collective-permute-start(bf16[128,384]{1,0:T(8,128)(2,1)S(1)} %bitcast.39), channel_id=1, source_target_pairs={{0,16},{32,48},{64,80},{96,112},{128,144},{160,176},{192,208},{224... | collective-permute-start | bytes 294920 | tf_op jit(solution)/shard_map/ppermute | solution.py:385

commit v4 on v3

--- a/solution.py
+++ b/solution.py
@@ -316,34 +316,33 @@
     act = act_ref[...].astype(F32)
     acc[...] = jnp.zeros(acc.shape, F32)
     for m in range(7):
-        acc[1, pl.ds(m, 16, stride=16), :] = total[:, 128 * m : 128 * m + 128]
+        acc[pl.ds(48 + m, 16, stride=56), :] = total[:, 128 * m : 128 * m + 128]
     for h in range(16):
         for side in range(2):
-            at = 16 * h + 8 * side
-            acc[0, at : at + 8, :] = act[8 * h : 8 * h + 8, 128 * side : 128 * side + 128]
-    out_ref[:, 256:384] = acc[0, 0:256, :].astype(BF)
-    out_ref[:, 384:512] = acc[1, 0:256, :].astype(BF)
-    one = total[:, 896:1152].astype(BF)
-    for h in range(16):
-        out_ref[16 * h : 16 * h + 16, 0:256] = one
+            at = 56 * h + 16 * side
+            acc[at : at + 16, :] = total[:, 896 + 128 * side : 1024 + 128 * side]
+            at = 56 * h + 32 + 8 * side
+            acc[at : at + 8, :] = act[8 * h : 8 * h + 8, 128 * side : 128 * side + 128]
+    out_ref[...] = acc[0:896, :].astype(BF)
 
 
 def sum_height_body(in_ref, out_ref):
-    one, two = None, None
-    for h in range(16):
-        block = in_ref[16 * h : 16 * h + 16, :].astype(F32)
-        one = block[:, 0:256] if h == 0 else one + block[:, 0:256]
-        two = block[:, 384:512] if h == 0 else two + block[:, 384:512]
-    packed = jnp.concatenate([one, two], axis=1).astype(BF)
+    value = in_ref[...].astype(F32)
+    total = value[0:56]
+    for h in range(1, 16):
+        total = total + value[56 * h : 56 * h + 56]
+    two = jnp.concatenate([total[48:56], jnp.zeros((8, 128), F32)], axis=0)
+    packed = jnp.concatenate([total[0:16], total[16:32], two], axis=1).astype(BF)
     for c in range(8):
         out_ref[16 * c : 16 * c + 16, :] = packed
 
 
 def lay_activation_body(in_ref, act_ref, acc):
+    rows = in_ref[...].astype(F32)
     for h in range(16):
-        block = in_ref[16 * h : 16 * h + 16, 256:384].astype(F32)
         for r in range(4):
-            value = block[8 * (r // 2) : 8 * (r // 2) + 8, :]
+            at = 56 * h + 32 + 8 * (r // 2)
+            value = rows[at : at + 8]
             acc[pl.ds(4 * h + r, 8, stride=64), :] = pltpu.roll(value, 64, 1) if r % 2 else value
     act_ref[...] = acc[0:512, :][:, 0:64].astype(BF)
 
@@ -475,9 +474,9 @@
     same_core = [list(range(core, lax.axis_size("dev"), 2)) for core in range(2)]
     (second,) = call(
         sum_depth_body,
-        [shape((256, 512), BF)],
+        [shape((896, 128), BF)],
         [exchange(first, "dev", same_core), act],
-        [pltpu.VMEM((2, 272, 128), F32)],
+        [pltpu.VMEM((960, 128), F32)],
     )
     second = exchange(second, "ha")
     (third,) = call(sum_height_body, [shape((128, 384), BF)], [second])

time: 105 us -> 104 us (level)
  no operation moved by 1% of the time
where the time goes in v4:
time: 104 us
  starting transfers between devices  41.9 us (40%)
  blocking collectives  41.3 us (40%)
  Pallas kernels  11.8 us (11%)
  waiting for transfers between devices  5.63 us (5%)
  local copies, waits for them, and re-layouts  2.17 us (2%)
    all_to_all x3, blocking collectives, exchange(): lax.all_to_all(block, axis, 0, 0, tiled=True, axis_index_groups=groups)  41.3 us
    ppermute x9, starting transfers between devices, swap(): return lax.ppermute(block, axis, pairs + [(j, i) for i, j in pairs])  16.6 us
    pallas_call x14, Pallas kernels, call(): pl.pallas_call(body, out_shape=out_shape, in_specs=[pl.BlockSpec(memory_s...  11.8 us
    all_to_all x1, starting transfers between devices, exchange(): lax.all_to_all(block, axis, 0, 0, tiled=True, axis_index_groups=groups)  11.6 us
    ppermute x2, starting transfers between devices, move(): lax.ppermute(block, axis, [(i, i + step) for i in range(size) if 0 <= i +...  7.93 us
    ppermute x9, waiting for transfers between devices, swap(): return lax.ppermute(block, axis, pairs + [(j, i) for i, j in pairs])  5.61 us
    ppermute x1, starting transfers between devices, shards(): lax.ppermute(corner, ('dev', 'ha'), [(d * n_ha + h, (d + 1) * n_ha + h +...  5.21 us
    unnamed x4, local copies, waits for them, and re-layouts  2.16 us
  transfers between devices with their start and end apart: 14, of which 5 were waited for; matrix products, arithmetic and copies ran while one was open for 0% of the time, Pallas kernels for 6%

profile of v4, /device:TPU:1, one launch (start us, length us, event | category | flops | bytes accessed | tf_op | source)
XLA Modules:
  0.0 103.7 jit_solution(16422975115026429608)
XLA Ops:
  0.6 2.3 %shard_map.76 = (bf16[512,256]{1,0:T(8,128)(2,1)}, bf16[128,256]{1,0:T(8,128)(2,1)}, bf16[32,256]{1,0:T(8,128)(2,1)}, bf16[128,1280]{1,0:T(8,128)(2,1)}) custom-call(bf16[2048,256]{1,0:T(8,128)(2,1)} %bitcast.28, bf16[27,8,64]{2,1,0:T(8,128)(2,1)} %bitcast.46, bf16[512,64]{1,0:T(8,128)(2,1)} %bitcast.44), custom_call_target="tpu_custom_call" | custom-call | flops 1000000 | bytes 1813504 | tf_op jit(solution)/shard_map/pallas_call | solution.py:19
  2.9 11.6 %all-to-all-start = ((bf16[16,8,1280]{2,1,0:T(8,128)(2,1)}), bf16[16,8,1280]{2,1,0:T(8,128)(2,1)S(1)}, u32[]{:S(2)}, u32[]{:S(2)}) async-start(bf16[16,8,1280]{2,1,0:T(8,128)(2,1)} %bitcast.43), calls=%async_computation | async-start | bytes 655360 | tf_op jit(solution)/shard_map/all_to_all | solution.py:388
  14.5 3.5 %collective-permute-start = (bf16[512,256]{1,0:T(8,128)(2,1)}, bf16[512,256]{1,0:T(8,128)(2,1)S(1)}, u32[]{:S(2)}, u32[]{:S(2)}) collective-permute-start(bf16[512,256]{1,0:T(8,128)(2,1)} %get-tuple-element.30), channel_id=1, source_target_pairs={{0,16},{16,32},{32,48},{48,64},{64,80},{80,96},{96,112},{112,128},... | collective-permute-start | bytes 786440 | tf_op jit(solution)/shard_map/ppermute | solution.py:379
  18.0 4.4 %collective-permute-start.1 = (bf16[128,256]{1,0:T(8,128)(2,1)}, bf16[128,256]{1,0:T(8,128)(2,1)S(1)}, u32[]{:S(2)}, u32[]{:S(2)}) collective-permute-start(bf16[128,256]{1,0:T(8,128)(2,1)} %get-tuple-element.31), channel_id=1, source_target_pairs={{0,1},{1,2},{2,3},{3,4},{4,5},{5,6},{6,7},{7,8},{8,9},{9,10},{10,1... | collective-permute-start | bytes 196616 | tf_op jit(solution)/shard_map/ppermute | solution.py:379
  22.5 5.2 %collective-permute-start.2 = (bf16[32,256]{1,0:T(8,128)(2,1)}, bf16[32,256]{1,0:T(8,128)(2,1)S(1)}, u32[]{:S(2)}, u32[]{:S(2)}) collective-permute-start(bf16[32,256]{1,0:T(8,128)(2,1)} %get-tuple-element.32), channel_id=1, source_target_pairs={{0,17},{1,18},{2,19},{3,20},{4,21},{5,22},{6,23},{7,24},{8,25},{9,... | collective-permute-start | bytes 49160 | tf_op jit(solution)/shard_map/ppermute | solution.py:415
  27.7 1.2 %copy-done = bf16[32,4,16,256]{3,2,1,0:T(8,128)(2,1)S(1)} copy-done((bf16[32,4,16,256]{3,2,1,0:T(8,128)(2,1)S(1)}, bf16[32,4,16,256]{3,2,1,0:T(8,128)(2,1)}, u32[]{:S(2)}) %copy-start) | copy-done | bytes 1048600
  28.9 0.9 copy-done.1
  29.9 1.7 %shard_map.75 = (bf16[64,96,128]{2,1,0:T(8,128)(2,1)S(1)}, bf16[64,864]{1,0:T(8,128)(2,1)S(1)}) custom-call(bf16[2048,256]{1,0:T(8,128)(2,1)S(1)} %bitcast.29, bf16[864,64]{1,0:T(8,128)(2,1)S(1)} %bitcast.42), custom_call_target="tpu_custom_call" | custom-call | flops 300000000 | bytes 2842624 | tf_op jit(solution)/shard_map/pallas_call | solution.py:19
  31.6 1.4 %shard_map.77 = (f32[64,2048]{1,0:T(8,128)S(1)}, bf16[64,256]{1,0:T(8,128)(2,1)S(1)}, bf16[16,96,128]{2,1,0:T(8,128)(2,1)S(1)}, bf16[5,96,128]{2,1,0:T(8,128)(2,1)S(1)}) custom-call(bf16[64,96,128]{2,1,0:T(8,128)(2,1)S(1)} %get-tuple-element.28.own_ref.image_ref, bf16[64,864]{1,0:T(8,128)(2,1)S(1)} %get-tuple-element.29.wt_ref, ...), custom_call_target="tpu_custom_call" | custom-call | flops 400000000 | bytes 3100672 | tf_op jit(solution)/shard_map/pallas_call | solution.py:19
  33.5 3.6 %collective-permute-start.6 = (bf16[128,384]{1,0:T(8,128)(2,1)S(1)}, bf16[128,384]{1,0:T(8,128)(2,1)S(1)}, u32[]{:S(2)}, u32[]{:S(2)}) collective-permute-start(bf16[128,384]{1,0:T(8,128)(2,1)S(1)} %slice.4), channel_id=1, source_target_pairs={{16,32},{48,64},{80,96},{112,128},{144,160},{176,192},{208,224},{3... | collective-permute-start | bytes 294920 | tf_op jit(solution)/shard_map/ppermute | solution.py:384
  37.9 3.6 %collective-permute-start.5 = (bf16[128,128]{1,0:T(8,128)(2,1)S(1)}, bf16[128,128]{1,0:T(8,128)(2,1)S(1)}, u32[]{:S(2)}, u32[]{:S(2)}) collective-permute-start(bf16[128,128]{1,0:T(8,128)(2,1)S(1)} %collective-permute-done.4.mine_ref), channel_id=1, source_target_pairs={{0,16},{32,48},{64,80},{96,112},{128,144},{160,176},{192,208},{224... | collective-permute-start | bytes 98312 | tf_op jit(solution)/shard_map/ppermute | solution.py:384
  41.5 0.9 collective-permute-done.5.core_ref
  42.4 4.7 %collective-permute-start.7 = (bf16[128,512]{1,0:T(8,128)(2,1)S(1)}, bf16[128,512]{1,0:T(8,128)(2,1)S(1)}, u32[]{:S(2)}, u32[]{:S(2)}) collective-permute-start(bf16[128,512]{1,0:T(8,128)(2,1)S(1)} %shard_map.79.pair_ref), channel_id=1, source_target_pairs={{16,32},{48,64},{80,96},{112,128},{144,160},{176,192},{208,224},{3... | collective-permute-start | bytes 393224 | tf_op jit(solution)/shard_map/ppermute | solution.py:384
  47.0 2.6 %collective-permute-done.7.cross_ref = bf16[128,512]{1,0:T(8,128)(2,1)S(1)} collective-permute-done((bf16[128,512]{1,0:T(8,128)(2,1)S(1)}, bf16[128,512]{1,0:T(8,128)(2,1)S(1)}, u32[]{:S(2)}, u32[]{:S(2)}) %collective-permute-start.7) | collective-permute-done | bytes 131104 | tf_op jit(solution)/shard_map/ppermute | solution.py:384
  49.9 1.1 %collective-permute-done.8.core_ref = bf16[128,512]{1,0:T(8,128)(2,1)S(1)} collective-permute-done((bf16[128,512]{1,0:T(8,128)(2,1)S(1)}, bf16[128,512]{1,0:T(8,128)(2,1)S(1)}, u32[]{:S(2)}, u32[]{:S(2)}) %collective-permute-start.8) | collective-permute-done | bytes 131104 | tf_op jit(solution)/shard_map/ppermute | solution.py:384
  51.0 1.3 %shard_map.81 = (bf16[2944,384]{1,0:T(8,128)(2,1)S(1)}, bf16[128,256]{1,0:T(8,128)(2,1)S(1)}, bf16[384,384]{1,0:T(8,128)(2,1)S(1)}) custom-call(bf16[128,512]{1,0:T(8,128)(2,1)S(1)} %shard_map.79.pair_ref, bf16[128,512]{1,0:T(8,128)(2,1)S(1)} %collective-permute-done.7.cross_ref, bf16[128,512]{1,0:T(8,128)(2,1)S(1)} %collective-permute-done.8.core_ref, ...), custom_call_target="tpu_custom_call" | custom-call | flops 500000000 | bytes 4227072 | tf_op jit(solution)/shard_map/pallas_call | solution.py:19
  53.2 2.2 %shard_map.83 = (bf16[64,4,64]{2,1,0:T(4,128)(2,1)}, f32[128,256]{1,0:T(8,128)S(1)}, bf16[128,256]{1,0:T(8,128)(2,1)S(1)}) custom-call(bf16[384,384]{1,0:T(8,128)(2,1)S(1)} %get-tuple-element.38.delta_ref, bf16[64,3456]{1,0:T(8,128)(2,1)S(1)} %get-tuple-element.42.wb_ref, f32[64,2048]{1,0:T(8,128)S(1)} %get-tuple-element.43.slope_ref, ...), custom_call_target="tpu_custom_call" | custom-call | flops 400000000 | bytes 3579904 | tf_op jit(solution)/shard_map/pallas_call | solution.py:19
  55.9 0.9 collective-permute-done.11.other_one_ref
  56.8 15.0 %all_to_all.44 = bf16[8,16,1152]{2,1,0:T(8,128)(2,1)S(1)} all-to-all(bf16[8,16,1152]{2,1,0:T(8,128)(2,1)S(1)} %bitcast.37), channel_id=1, replica_groups={{0,32,64,96,128,160,192,224},{16,48,80,112,144,176,208,240},{1,33,65,97..., dimensions={0} | all-to-all | bytes 589824 | tf_op jit(solution)/shard_map/all_to_all | solution.py:388
  71.8 18.6 %all_to_all.45 = bf16[16,56,128]{2,1,0:T(8,128)(2,1)S(1)} all-to-all(bf16[16,56,128]{2,1,0:T(8,128)(2,1)S(1)} %bitcast.38), channel_id=1, replica_groups=mesh['dev'=16,'ha'=16] {'ha'}, dimensions={0} | all-to-all | bytes 458752 | tf_op jit(solution)/shard_map/all_to_all | solution.py:388
  90.5 7.8 %all_to_all.46 = bf16[8,16,384]{2,1,0:T(8,128)(2,1)S(1)} all-to-all(bf16[8,16,384]{2,1,0:T(8,128)(2,1)S(1)} %bitcast.41), channel_id=1, replica_groups={{0,32,64,96,128,160,192,224},{16,48,80,112,144,176,208,240},{1,33,65,97..., dimensions={0} | all-to-all | bytes 196608 | tf_op jit(solution)/shard_map/all_to_all | solution.py:388
  98.3 3.5 %collective-permute-start.12 = (bf16[128,384]{1,0:T(8,128)(2,1)S(1)}, bf16[128,384]{1,0:T(8,128)(2,1)S(1)}, u32[]{:S(2)}, u32[]{:S(2)}) collective-permute-start(bf16[128,384]{1,0:T(8,128)(2,1)S(1)} %bitcast.39), channel_id=1, source_target_pairs={{0,16},{32,48},{64,80},{96,112},{128,144},{160,176},{192,208},{224... | collective-permute-start | bytes 294920 | tf_op jit(solution)/shard_map/ppermute | solution.py:384
  101.7 0.8 shard_map.86
  102.7 1.0 shard_map.88
  (26 shorter events, 3.1 us)
Async XLA Ops:
  2.9 30.5 %all-to-all-start = ((bf16[16,8,1280]{2,1,0:T(8,128)(2,1)}), bf16[16,8,1280]{2,1,0:T(8,128)(2,1)S(1)}, u32[]{:S(2)}, u32[]{:S(2)}) async-start(bf16[16,8,1280]{2,1,0:T(8,128)(2,1)} %bitcast.43), calls=%async_computation | async-start | bytes 655360 | tf_op jit(solution)/shard_map/all_to_all | solution.py:388
  14.5 17.1 %collective-permute-start = (bf16[512,256]{1,0:T(8,128)(2,1)}, bf16[512,256]{1,0:T(8,128)(2,1)S(1)}, u32[]{:S(2)}, u32[]{:S(2)}) collective-permute-start(bf16[512,256]{1,0:T(8,128)(2,1)} %get-tuple-element.30), channel_id=1, source_target_pairs={{0,16},{16,32},{32,48},{48,64},{64,80},{80,96},{96,112},{112,128},... | collective-permute-start | bytes 786440 | tf_op jit(solution)/shard_map/ppermute | solution.py:379
  18.0 13.5 %collective-permute-start.1 = (bf16[128,256]{1,0:T(8,128)(2,1)}, bf16[128,256]{1,0:T(8,128)(2,1)S(1)}, u32[]{:S(2)}, u32[]{:S(2)}) collective-permute-start(bf16[128,256]{1,0:T(8,128)(2,1)} %get-tuple-element.31), channel_id=1, source_target_pairs={{0,1},{1,2},{2,3},{3,4},{4,5},{5,6},{6,7},{7,8},{8,9},{9,10},{10,1... | collective-permute-start | bytes 196616 | tf_op jit(solution)/shard_map/ppermute | solution.py:379
  22.5 9.1 %collective-permute-start.2 = (bf16[32,256]{1,0:T(8,128)(2,1)}, bf16[32,256]{1,0:T(8,128)(2,1)S(1)}, u32[]{:S(2)}, u32[]{:S(2)}) collective-permute-start(bf16[32,256]{1,0:T(8,128)(2,1)} %get-tuple-element.32), channel_id=1, source_target_pairs={{0,17},{1,18},{2,19},{3,20},{4,21},{5,22},{6,23},{7,24},{8,25},{9,... | collective-permute-start | bytes 49160 | tf_op jit(solution)/shard_map/ppermute | solution.py:415
  27.7 1.2 %copy-start = (bf16[32,4,16,256]{3,2,1,0:T(8,128)(2,1)S(1)}, bf16[32,4,16,256]{3,2,1,0:T(8,128)(2,1)}, u32[]{:S(2)}) copy-start(bf16[32,4,16,256]{3,2,1,0:T(8,128)(2,1)} %param.4) | copy-start | bytes 3145732
  28.9 0.9 copy-start.1
  33.0 4.1 %collective-permute-start.3 = (bf16[64,256]{1,0:T(8,128)(2,1)S(1)}, bf16[64,256]{1,0:T(8,128)(2,1)S(1)}, u32[]{:S(2)}, u32[]{:S(2)}) collective-permute-start(bf16[64,256]{1,0:T(8,128)(2,1)S(1)} %get-tuple-element.33.own_ref), channel_id=1, source_target_pairs={{0,16},{32,48},{64,80},{96,112},{128,144},{160,176},{192,208},{224... | collective-permute-start | bytes 98312 | tf_op jit(solution)/shard_map/ppermute | solution.py:384
  33.5 8.9 %collective-permute-start.6 = (bf16[128,384]{1,0:T(8,128)(2,1)S(1)}, bf16[128,384]{1,0:T(8,128)(2,1)S(1)}, u32[]{:S(2)}, u32[]{:S(2)}) collective-permute-start(bf16[128,384]{1,0:T(8,128)(2,1)S(1)} %slice.4), channel_id=1, source_target_pairs={{16,32},{48,64},{80,96},{112,128},{144,160},{176,192},{208,224},{3... | collective-permute-start | bytes 294920 | tf_op jit(solution)/shard_map/ppermute | solution.py:384
  37.1 0.8 collective-permute-start.4
  37.7 11.9 %collective-permute-start.9 = (bf16[128,1280]{1,0:T(8,128)(2,1)S(1)}, bf16[128,1280]{1,0:T(8,128)(2,1)S(1)}, u32[]{:S(2)}, u32[]{:S(2)}) collective-permute-start(bf16[128,1280]{1,0:T(8,128)(2,1)S(1)} %bitcast.33), channel_id=1, source_target_pairs={{0,16},{32,48},{64,80},{96,112},{128,144},{160,176},{192,208},{224... | collective-permute-start | bytes 983048 | tf_op jit(solution)/shard_map/ppermute | solution.py:384
  37.9 4.5 %collective-permute-start.5 = (bf16[128,128]{1,0:T(8,128)(2,1)S(1)}, bf16[128,128]{1,0:T(8,128)(2,1)S(1)}, u32[]{:S(2)}, u32[]{:S(2)}) collective-permute-start(bf16[128,128]{1,0:T(8,128)(2,1)S(1)} %collective-permute-done.4.mine_ref), channel_id=1, source_target_pairs={{0,16},{32,48},{64,80},{96,112},{128,144},{160,176},{192,208},{224... | collective-permute-start | bytes 98312 | tf_op jit(solution)/shard_map/ppermute | solution.py:384
  42.4 7.3 %collective-permute-start.7 = (bf16[128,512]{1,0:T(8,128)(2,1)S(1)}, bf16[128,512]{1,0:T(8,128)(2,1)S(1)}, u32[]{:S(2)}, u32[]{:S(2)}) collective-permute-start(bf16[128,512]{1,0:T(8,128)(2,1)S(1)} %shard_map.79.pair_ref), channel_id=1, source_target_pairs={{16,32},{48,64},{80,96},{112,128},{144,160},{176,192},{208,224},{3... | collective-permute-start | bytes 393224 | tf_op jit(solution)/shard_map/ppermute | solution.py:384
  49.7 1.3 %collective-permute-start.8 = (bf16[128,512]{1,0:T(8,128)(2,1)S(1)}, bf16[128,512]{1,0:T(8,128)(2,1)S(1)}, u32[]{:S(2)}, u32[]{:S(2)}) collective-permute-start(bf16[128,512]{1,0:T(8,128)(2,1)S(1)} %collective-permute-done.7.cross_ref), channel_id=1, source_target_pairs={{0,16},{32,48},{64,80},{96,112},{128,144},{160,176},{192,208},{224... | collective-permute-start | bytes 393224 | tf_op jit(solution)/shard_map/ppermute | solution.py:384
  53.0 3.8 %collective-permute-start.10 = (bf16[128,896]{1,0:T(8,128)(2,1)S(1)}, bf16[128,896]{1,0:T(8,128)(2,1)S(1)}, u32[]{:S(2)}, u32[]{:S(2)}) collective-permute-start(bf16[128,896]{1,0:T(8,128)(2,1)S(1)} %get-tuple-element.41), channel_id=1, source_target_pairs={{0,16},{32,48},{64,80},{96,112},{128,144},{160,176},{192,208},{224... | collective-permute-start | bytes 688136 | tf_op jit(solution)/shard_map/ppermute | solution.py:384
  55.4 1.3 %collective-permute-start.11 = (bf16[128,256]{1,0:T(8,128)(2,1)S(1)}, bf16[128,256]{1,0:T(8,128)(2,1)S(1)}, u32[]{:S(2)}, u32[]{:S(2)}) collective-permute-start(bf16[128,256]{1,0:T(8,128)(2,1)S(1)} %get-tuple-element.47), channel_id=1, source_target_pairs={{0,16},{32,48},{64,80},{96,112},{128,144},{160,176},{192,208},{224... | collective-permute-start | bytes 196616 | tf_op jit(solution)/shard_map/ppermute | solution.py:384
  98.3 4.4 %collective-permute-start.12 = (bf16[128,384]{1,0:T(8,128)(2,1)S(1)}, bf16[128,384]{1,0:T(8,128)(2,1)S(1)}, u32[]{:S(2)}, u32[]{:S(2)}) collective-permute-start(bf16[128,384]{1,0:T(8,128)(2,1)S(1)} %bitcast.39), channel_id=1, source_target_pairs={{0,16},{32,48},{64,80},{96,112},{128,144},{160,176},{192,208},{224... | collective-permute-start | bytes 294920 | tf_op jit(solution)/shard_map/ppermute | solution.py:384

commit v5 on v4

--- a/solution.py
+++ b/solution.py
@@ -331,10 +331,8 @@
     total = value[0:56]
     for h in range(1, 16):
         total = total + value[56 * h : 56 * h + 56]
-    two = jnp.concatenate([total[48:56], jnp.zeros((8, 128), F32)], axis=0)
-    packed = jnp.concatenate([total[0:16], total[16:32], two], axis=1).astype(BF)
-    for c in range(8):
-        out_ref[16 * c : 16 * c + 16, :] = packed
+    packed = jnp.concatenate([total[0:32], total[48:56]], axis=0)
+    out_ref[...] = jnp.concatenate([packed] * 8, axis=0).astype(BF)
 
 
 def lay_activation_body(in_ref, act_ref, acc):
@@ -349,13 +347,13 @@
 
 def finish_body(mine_ref, other_ref, one_ref, two_ref, acc):
     even = is_even("dev")
+    mine, other = mine_ref[...].astype(F32), other_ref[...].astype(F32)
+    first, second = jnp.where(even, mine, other), jnp.where(even, other, mine)
     for c in range(8):
-        mine = mine_ref[16 * c : 16 * c + 16, :].astype(F32)
-        other = other_ref[16 * c : 16 * c + 16, :].astype(F32)
-        first, second = jnp.where(even, mine, other), jnp.where(even, other, mine)
-        for part in range(3):
-            acc[part, 32 * c : 32 * c + 16, :] = first[:, 128 * part : 128 * part + 128]
-            acc[part, 32 * c + 16 : 32 * c + 32, :] = second[:, 128 * part : 128 * part + 128]
+        for part, count in enumerate((16, 16, 8)):
+            at = 40 * c + 16 * part
+            acc[part, 32 * c : 32 * c + count, :] = first[at : at + count]
+            acc[part, 32 * c + 16 : 32 * c + 16 + count, :] = second[at : at + count]
     for half in range(2):
         for m in range(7):
             value = acc[2, pl.ds(16 * half + m, 8, stride=32), :] * (1.0 / math.sqrt(CELLS_TWO))
@@ -479,7 +477,7 @@
         [pltpu.VMEM((960, 128), F32)],
     )
     second = exchange(second, "ha")
-    (third,) = call(sum_height_body, [shape((128, 384), BF)], [second])
+    (third,) = call(sum_height_body, [shape((320, 128), BF)], [second])
     (activation,) = call(lay_activation_body, [shape((512, 64), BF)], [second], [pltpu.VMEM((576, 128), F32)])
     third = exchange(third, "dev", same_core)
     one, two = call(

time: 104 us -> 104 us (level)
  no operation moved by 1% of the time
where the time goes in v5:
time: 104 us
  starting transfers between devices  42 us (40%)
  blocking collectives  41.2 us (40%)
  Pallas kernels  11.8 us (11%)
  waiting for transfers between devices  5.61 us (5%)
  local copies, waits for them, and re-layouts  2.17 us (2%)
    all_to_all x3, blocking collectives, exchange(): lax.all_to_all(block, axis, 0, 0, tiled=True, axis_index_groups=groups)  41.2 us
    ppermute x9, starting transfers between devices, swap(): return lax.ppermute(block, axis, pairs + [(j, i) for i, j in pairs])  16.6 us
    pallas_call x14, Pallas kernels, call(): pl.pallas_call(body, out_shape=out_shape, in_specs=[pl.BlockSpec(memory_s...  11.8 us
    all_to_all x1, starting transfers between devices, exchange(): lax.all_to_all(block, axis, 0, 0, tiled=True, axis_index_groups=groups)  11.6 us
    ppermute x2, starting transfers between devices, move(): lax.ppermute(block, axis, [(i, i + step) for i in range(size) if 0 <= i +...  7.93 us
    ppermute x9, waiting for transfers between devices, swap(): return lax.ppermute(block, axis, pairs + [(j, i) for i, j in pairs])  5.59 us
    ppermute x1, starting transfers between devices, shards(): lax.ppermute(corner, ('dev', 'ha'), [(d * n_ha + h, (d + 1) * n_ha + h +...  5.21 us
    unnamed x4, local copies, waits for them, and re-layouts  2.16 us
  transfers between devices with their start and end apart: 14, of which 5 were waited for; matrix products, arithmetic and copies ran while one was open for 0% of the time, Pallas kernels for 6%

profile of v5, /device:TPU:1, one launch (start us, length us, event | category | flops | bytes accessed | tf_op | source)
XLA Modules:
  0.0 103.6 jit_solution(6400442919338250871)
XLA Ops:
  0.6 2.3 %shard_map.76 = (bf16[512,256]{1,0:T(8,128)(2,1)}, bf16[128,256]{1,0:T(8,128)(2,1)}, bf16[32,256]{1,0:T(8,128)(2,1)}, bf16[128,1280]{1,0:T(8,128)(2,1)}) custom-call(bf16[2048,256]{1,0:T(8,128)(2,1)} %bitcast.28, bf16[27,8,64]{2,1,0:T(8,128)(2,1)} %bitcast.46, bf16[512,64]{1,0:T(8,128)(2,1)} %bitcast.44), custom_call_target="tpu_custom_call" | custom-call | flops 1000000 | bytes 1813504 | tf_op jit(solution)/shard_map/pallas_call | solution.py:19
  2.9 11.6 %all-to-all-start = ((bf16[16,8,1280]{2,1,0:T(8,128)(2,1)}), bf16[16,8,1280]{2,1,0:T(8,128)(2,1)S(1)}, u32[]{:S(2)}, u32[]{:S(2)}) async-start(bf16[16,8,1280]{2,1,0:T(8,128)(2,1)} %bitcast.43), calls=%async_computation | async-start | bytes 655360 | tf_op jit(solution)/shard_map/all_to_all | solution.py:386
  14.5 3.5 %collective-permute-start = (bf16[512,256]{1,0:T(8,128)(2,1)}, bf16[512,256]{1,0:T(8,128)(2,1)S(1)}, u32[]{:S(2)}, u32[]{:S(2)}) collective-permute-start(bf16[512,256]{1,0:T(8,128)(2,1)} %get-tuple-element.30), channel_id=1, source_target_pairs={{0,16},{16,32},{32,48},{48,64},{64,80},{80,96},{96,112},{112,128},... | collective-permute-start | bytes 786440 | tf_op jit(solution)/shard_map/ppermute | solution.py:377
  18.0 4.4 %collective-permute-start.1 = (bf16[128,256]{1,0:T(8,128)(2,1)}, bf16[128,256]{1,0:T(8,128)(2,1)S(1)}, u32[]{:S(2)}, u32[]{:S(2)}) collective-permute-start(bf16[128,256]{1,0:T(8,128)(2,1)} %get-tuple-element.31), channel_id=1, source_target_pairs={{0,1},{1,2},{2,3},{3,4},{4,5},{5,6},{6,7},{7,8},{8,9},{9,10},{10,1... | collective-permute-start | bytes 196616 | tf_op jit(solution)/shard_map/ppermute | solution.py:377
  22.5 5.2 %collective-permute-start.2 = (bf16[32,256]{1,0:T(8,128)(2,1)}, bf16[32,256]{1,0:T(8,128)(2,1)S(1)}, u32[]{:S(2)}, u32[]{:S(2)}) collective-permute-start(bf16[32,256]{1,0:T(8,128)(2,1)} %get-tuple-element.32), channel_id=1, source_target_pairs={{0,17},{1,18},{2,19},{3,20},{4,21},{5,22},{6,23},{7,24},{8,25},{9,... | collective-permute-start | bytes 49160 | tf_op jit(solution)/shard_map/ppermute | solution.py:413
  27.7 1.2 %copy-done = bf16[32,4,16,256]{3,2,1,0:T(8,128)(2,1)S(1)} copy-done((bf16[32,4,16,256]{3,2,1,0:T(8,128)(2,1)S(1)}, bf16[32,4,16,256]{3,2,1,0:T(8,128)(2,1)}, u32[]{:S(2)}) %copy-start) | copy-done | bytes 1048600
  28.9 0.9 copy-done.1
  29.9 1.7 %shard_map.75 = (bf16[64,96,128]{2,1,0:T(8,128)(2,1)S(1)}, bf16[64,864]{1,0:T(8,128)(2,1)S(1)}) custom-call(bf16[2048,256]{1,0:T(8,128)(2,1)S(1)} %bitcast.29, bf16[864,64]{1,0:T(8,128)(2,1)S(1)} %bitcast.42), custom_call_target="tpu_custom_call" | custom-call | flops 300000000 | bytes 2842624 | tf_op jit(solution)/shard_map/pallas_call | solution.py:19
  31.6 1.4 %shard_map.77 = (f32[64,2048]{1,0:T(8,128)S(1)}, bf16[64,256]{1,0:T(8,128)(2,1)S(1)}, bf16[16,96,128]{2,1,0:T(8,128)(2,1)S(1)}, bf16[5,96,128]{2,1,0:T(8,128)(2,1)S(1)}) custom-call(bf16[64,96,128]{2,1,0:T(8,128)(2,1)S(1)} %get-tuple-element.28.own_ref.image_ref, bf16[64,864]{1,0:T(8,128)(2,1)S(1)} %get-tuple-element.29.wt_ref, ...), custom_call_target="tpu_custom_call" | custom-call | flops 400000000 | bytes 3100672 | tf_op jit(solution)/shard_map/pallas_call | solution.py:19
  33.5 3.6 %collective-permute-start.6 = (bf16[128,384]{1,0:T(8,128)(2,1)S(1)}, bf16[128,384]{1,0:T(8,128)(2,1)S(1)}, u32[]{:S(2)}, u32[]{:S(2)}) collective-permute-start(bf16[128,384]{1,0:T(8,128)(2,1)S(1)} %slice.4), channel_id=1, source_target_pairs={{16,32},{48,64},{80,96},{112,128},{144,160},{176,192},{208,224},{3... | collective-permute-start | bytes 294920 | tf_op jit(solution)/shard_map/ppermute | solution.py:382
  37.9 3.6 %collective-permute-start.5 = (bf16[128,128]{1,0:T(8,128)(2,1)S(1)}, bf16[128,128]{1,0:T(8,128)(2,1)S(1)}, u32[]{:S(2)}, u32[]{:S(2)}) collective-permute-start(bf16[128,128]{1,0:T(8,128)(2,1)S(1)} %collective-permute-done.4.mine_ref), channel_id=1, source_target_pairs={{0,16},{32,48},{64,80},{96,112},{128,144},{160,176},{192,208},{224... | collective-permute-start | bytes 98312 | tf_op jit(solution)/shard_map/ppermute | solution.py:382
  41.5 0.9 collective-permute-done.5.core_ref
  42.4 4.7 %collective-permute-start.7 = (bf16[128,512]{1,0:T(8,128)(2,1)S(1)}, bf16[128,512]{1,0:T(8,128)(2,1)S(1)}, u32[]{:S(2)}, u32[]{:S(2)}) collective-permute-start(bf16[128,512]{1,0:T(8,128)(2,1)S(1)} %shard_map.79.pair_ref), channel_id=1, source_target_pairs={{16,32},{48,64},{80,96},{112,128},{144,160},{176,192},{208,224},{3... | collective-permute-start | bytes 393224 | tf_op jit(solution)/shard_map/ppermute | solution.py:382
  47.0 2.6 %collective-permute-done.7.cross_ref = bf16[128,512]{1,0:T(8,128)(2,1)S(1)} collective-permute-done((bf16[128,512]{1,0:T(8,128)(2,1)S(1)}, bf16[128,512]{1,0:T(8,128)(2,1)S(1)}, u32[]{:S(2)}, u32[]{:S(2)}) %collective-permute-start.7) | collective-permute-done | bytes 131104 | tf_op jit(solution)/shard_map/ppermute | solution.py:382
  49.9 1.1 %collective-permute-done.8.core_ref = bf16[128,512]{1,0:T(8,128)(2,1)S(1)} collective-permute-done((bf16[128,512]{1,0:T(8,128)(2,1)S(1)}, bf16[128,512]{1,0:T(8,128)(2,1)S(1)}, u32[]{:S(2)}, u32[]{:S(2)}) %collective-permute-start.8) | collective-permute-done | bytes 131104 | tf_op jit(solution)/shard_map/ppermute | solution.py:382
  51.0 1.3 %shard_map.81 = (bf16[2944,384]{1,0:T(8,128)(2,1)S(1)}, bf16[128,256]{1,0:T(8,128)(2,1)S(1)}, bf16[384,384]{1,0:T(8,128)(2,1)S(1)}) custom-call(bf16[128,512]{1,0:T(8,128)(2,1)S(1)} %shard_map.79.pair_ref, bf16[128,512]{1,0:T(8,128)(2,1)S(1)} %collective-permute-done.7.cross_ref, bf16[128,512]{1,0:T(8,128)(2,1)S(1)} %collective-permute-done.8.core_ref, ...), custom_call_target="tpu_custom_call" | custom-call | flops 500000000 | bytes 4227072 | tf_op jit(solution)/shard_map/pallas_call | solution.py:19
  53.2 2.2 %shard_map.83 = (bf16[64,4,64]{2,1,0:T(4,128)(2,1)}, f32[128,256]{1,0:T(8,128)S(1)}, bf16[128,256]{1,0:T(8,128)(2,1)S(1)}) custom-call(bf16[384,384]{1,0:T(8,128)(2,1)S(1)} %get-tuple-element.38.delta_ref, bf16[64,3456]{1,0:T(8,128)(2,1)S(1)} %get-tuple-element.42.wb_ref, f32[64,2048]{1,0:T(8,128)S(1)} %get-tuple-element.43.slope_ref, ...), custom_call_target="tpu_custom_call" | custom-call | flops 400000000 | bytes 3579904 | tf_op jit(solution)/shard_map/pallas_call | solution.py:19
  55.9 0.9 collective-permute-done.11.other_one_ref
  56.8 15.0 %all_to_all.44 = bf16[8,16,1152]{2,1,0:T(8,128)(2,1)S(1)} all-to-all(bf16[8,16,1152]{2,1,0:T(8,128)(2,1)S(1)} %bitcast.37), channel_id=1, replica_groups={{0,32,64,96,128,160,192,224},{16,48,80,112,144,176,208,240},{1,33,65,97..., dimensions={0} | all-to-all | bytes 589824 | tf_op jit(solution)/shard_map/all_to_all | solution.py:386
  71.8 18.6 %all_to_all.45 = bf16[16,56,128]{2,1,0:T(8,128)(2,1)S(1)} all-to-all(bf16[16,56,128]{2,1,0:T(8,128)(2,1)S(1)} %bitcast.38), channel_id=1, replica_groups=mesh['dev'=16,'ha'=16] {'ha'}, dimensions={0} | all-to-all | bytes 458752 | tf_op jit(solution)/shard_map/all_to_all | solution.py:386
  90.5 7.7 %all_to_all.46 = bf16[8,40,128]{2,1,0:T(8,128)(2,1)S(1)} all-to-all(bf16[8,40,128]{2,1,0:T(8,128)(2,1)S(1)} %bitcast.41), channel_id=1, replica_groups={{0,32,64,96,128,160,192,224},{16,48,80,112,144,176,208,240},{1,33,65,97..., dimensions={0} | all-to-all | bytes 163840 | tf_op jit(solution)/shard_map/all_to_all | solution.py:386
  98.1 3.5 %collective-permute-start.12 = (bf16[320,128]{1,0:T(8,128)(2,1)S(1)}, bf16[320,128]{1,0:T(8,128)(2,1)S(1)}, u32[]{:S(2)}, u32[]{:S(2)}) collective-permute-start(bf16[320,128]{1,0:T(8,128)(2,1)S(1)} %bitcast.39), channel_id=1, source_target_pairs={{0,16},{32,48},{64,80},{96,112},{128,144},{160,176},{192,208},{224... | collective-permute-start | bytes 245768 | tf_op jit(solution)/shard_map/ppermute | solution.py:382
  101.6 0.8 shard_map.86
  102.6 1.0 shard_map.88
  (26 shorter events, 3.1 us)
Async XLA Ops:
  2.9 30.5 %all-to-all-start = ((bf16[16,8,1280]{2,1,0:T(8,128)(2,1)}), bf16[16,8,1280]{2,1,0:T(8,128)(2,1)S(1)}, u32[]{:S(2)}, u32[]{:S(2)}) async-start(bf16[16,8,1280]{2,1,0:T(8,128)(2,1)} %bitcast.43), calls=%async_computation | async-start | bytes 655360 | tf_op jit(solution)/shard_map/all_to_all | solution.py:386
  14.5 17.1 %collective-permute-start = (bf16[512,256]{1,0:T(8,128)(2,1)}, bf16[512,256]{1,0:T(8,128)(2,1)S(1)}, u32[]{:S(2)}, u32[]{:S(2)}) collective-permute-start(bf16[512,256]{1,0:T(8,128)(2,1)} %get-tuple-element.30), channel_id=1, source_target_pairs={{0,16},{16,32},{32,48},{48,64},{64,80},{80,96},{96,112},{112,128},... | collective-permute-start | bytes 786440 | tf_op jit(solution)/shard_map/ppermute | solution.py:377
  18.0 13.5 %collective-permute-start.1 = (bf16[128,256]{1,0:T(8,128)(2,1)}, bf16[128,256]{1,0:T(8,128)(2,1)S(1)}, u32[]{:S(2)}, u32[]{:S(2)}) collective-permute-start(bf16[128,256]{1,0:T(8,128)(2,1)} %get-tuple-element.31), channel_id=1, source_target_pairs={{0,1},{1,2},{2,3},{3,4},{4,5},{5,6},{6,7},{7,8},{8,9},{9,10},{10,1... | collective-permute-start | bytes 196616 | tf_op jit(solution)/shard_map/ppermute | solution.py:377
  22.5 9.1 %collective-permute-start.2 = (bf16[32,256]{1,0:T(8,128)(2,1)}, bf16[32,256]{1,0:T(8,128)(2,1)S(1)}, u32[]{:S(2)}, u32[]{:S(2)}) collective-permute-start(bf16[32,256]{1,0:T(8,128)(2,1)} %get-tuple-element.32), channel_id=1, source_target_pairs={{0,17},{1,18},{2,19},{3,20},{4,21},{5,22},{6,23},{7,24},{8,25},{9,... | collective-permute-start | bytes 49160 | tf_op jit(solution)/shard_map/ppermute | solution.py:413
  27.7 1.2 %copy-start = (bf16[32,4,16,256]{3,2,1,0:T(8,128)(2,1)S(1)}, bf16[32,4,16,256]{3,2,1,0:T(8,128)(2,1)}, u32[]{:S(2)}) copy-start(bf16[32,4,16,256]{3,2,1,0:T(8,128)(2,1)} %param.4) | copy-start | bytes 3145732
  28.9 0.9 copy-start.1
  33.0 4.1 %collective-permute-start.3 = (bf16[64,256]{1,0:T(8,128)(2,1)S(1)}, bf16[64,256]{1,0:T(8,128)(2,1)S(1)}, u32[]{:S(2)}, u32[]{:S(2)}) collective-permute-start(bf16[64,256]{1,0:T(8,128)(2,1)S(1)} %get-tuple-element.33.own_ref), channel_id=1, source_target_pairs={{0,16},{32,48},{64,80},{96,112},{128,144},{160,176},{192,208},{224... | collective-permute-start | bytes 98312 | tf_op jit(solution)/shard_map/ppermute | solution.py:382
  33.5 8.9 %collective-permute-start.6 = (bf16[128,384]{1,0:T(8,128)(2,1)S(1)}, bf16[128,384]{1,0:T(8,128)(2,1)S(1)}, u32[]{:S(2)}, u32[]{:S(2)}) collective-permute-start(bf16[128,384]{1,0:T(8,128)(2,1)S(1)} %slice.4), channel_id=1, source_target_pairs={{16,32},{48,64},{80,96},{112,128},{144,160},{176,192},{208,224},{3... | collective-permute-start | bytes 294920 | tf_op jit(solution)/shard_map/ppermute | solution.py:382
  37.1 0.8 collective-permute-start.4
  37.7 11.9 %collective-permute-start.9 = (bf16[128,1280]{1,0:T(8,128)(2,1)S(1)}, bf16[128,1280]{1,0:T(8,128)(2,1)S(1)}, u32[]{:S(2)}, u32[]{:S(2)}) collective-permute-start(bf16[128,1280]{1,0:T(8,128)(2,1)S(1)} %bitcast.33), channel_id=1, source_target_pairs={{0,16},{32,48},{64,80},{96,112},{128,144},{160,176},{192,208},{224... | collective-permute-start | bytes 983048 | tf_op jit(solution)/shard_map/ppermute | solution.py:382
  37.9 4.5 %collective-permute-start.5 = (bf16[128,128]{1,0:T(8,128)(2,1)S(1)}, bf16[128,128]{1,0:T(8,128)(2,1)S(1)}, u32[]{:S(2)}, u32[]{:S(2)}) collective-permute-start(bf16[128,128]{1,0:T(8,128)(2,1)S(1)} %collective-permute-done.4.mine_ref), channel_id=1, source_target_pairs={{0,16},{32,48},{64,80},{96,112},{128,144},{160,176},{192,208},{224... | collective-permute-start | bytes 98312 | tf_op jit(solution)/shard_map/ppermute | solution.py:382
  42.4 7.3 %collective-permute-start.7 = (bf16[128,512]{1,0:T(8,128)(2,1)S(1)}, bf16[128,512]{1,0:T(8,128)(2,1)S(1)}, u32[]{:S(2)}, u32[]{:S(2)}) collective-permute-start(bf16[128,512]{1,0:T(8,128)(2,1)S(1)} %shard_map.79.pair_ref), channel_id=1, source_target_pairs={{16,32},{48,64},{80,96},{112,128},{144,160},{176,192},{208,224},{3... | collective-permute-start | bytes 393224 | tf_op jit(solution)/shard_map/ppermute | solution.py:382
  49.7 1.3 %collective-permute-start.8 = (bf16[128,512]{1,0:T(8,128)(2,1)S(1)}, bf16[128,512]{1,0:T(8,128)(2,1)S(1)}, u32[]{:S(2)}, u32[]{:S(2)}) collective-permute-start(bf16[128,512]{1,0:T(8,128)(2,1)S(1)} %collective-permute-done.7.cross_ref), channel_id=1, source_target_pairs={{0,16},{32,48},{64,80},{96,112},{128,144},{160,176},{192,208},{224... | collective-permute-start | bytes 393224 | tf_op jit(solution)/shard_map/ppermute | solution.py:382
  53.0 3.8 %collective-permute-start.10 = (bf16[128,896]{1,0:T(8,128)(2,1)S(1)}, bf16[128,896]{1,0:T(8,128)(2,1)S(1)}, u32[]{:S(2)}, u32[]{:S(2)}) collective-permute-start(bf16[128,896]{1,0:T(8,128)(2,1)S(1)} %get-tuple-element.41), channel_id=1, source_target_pairs={{0,16},{32,48},{64,80},{96,112},{128,144},{160,176},{192,208},{224... | collective-permute-start | bytes 688136 | tf_op jit(solution)/shard_map/ppermute | solution.py:382
  55.4 1.3 %collective-permute-start.11 = (bf16[128,256]{1,0:T(8,128)(2,1)S(1)}, bf16[128,256]{1,0:T(8,128)(2,1)S(1)}, u32[]{:S(2)}, u32[]{:S(2)}) collective-permute-start(bf16[128,256]{1,0:T(8,128)(2,1)S(1)} %get-tuple-element.47), channel_id=1, source_target_pairs={{0,16},{32,48},{64,80},{96,112},{128,144},{160,176},{192,208},{224... | collective-permute-start | bytes 196616 | tf_op jit(solution)/shard_map/ppermute | solution.py:382
  98.1 4.4 %collective-permute-start.12 = (bf16[320,128]{1,0:T(8,128)(2,1)S(1)}, bf16[320,128]{1,0:T(8,128)(2,1)S(1)}, u32[]{:S(2)}, u32[]{:S(2)}) collective-permute-start(bf16[320,128]{1,0:T(8,128)(2,1)S(1)} %bitcast.39), channel_id=1, source_target_pairs={{0,16},{32,48},{64,80},{96,112},{128,144},{160,176},{192,208},{224... | collective-permute-start | bytes 245768 | tf_op jit(solution)/shard_map/ppermute | solution.py:382
